TPU v7x, 256 devices: a whole 4x4x8 slice. The times are simulated.
256 devices in a mesh: head: 8 (over z_hi, core), inner: 4 (over y), outer: 8 (over z_lo, x).
Axes of the slice: x: 4, y: 4, z: 8 (z_hi: 4, z_lo: 2; z = z_hi * 2 + z_lo), core: 2. Of those that a mesh axis runs over, the one named last changes fastest.
Arguments:
- queries: bfloat16 [7680, 4096], P(('inner', 'outer', 'head')), may hold values from -8 to 8
- keys: bfloat16 [7680, 1024], P(('inner', 'outer', 'head')), may hold values from -8 to 8
- values: bfloat16 [7680, 1024], P(('inner', 'outer', 'head')), may hold values from -6 to 6
- grad_out: bfloat16 [7680, 4096], P(('inner', 'outer', 'head')), may hold values from -6 to 6
- doc_lengths: int32 [16], replicated, may hold values from 1 to 768, 7680 in all
- positions: int32 [7680], replicated, may hold values from 0 to 7679, as said below
Outputs:
- attention: bfloat16 [7680, 4096], P(('inner', 'outer', 'head'))
- grad_queries: bfloat16 [7680, 4096], P(('inner', 'outer', 'head'))
- grad_keys: bfloat16 [7680, 1024], P(('inner', 'outer', 'head'))
- grad_values: bfloat16 [7680, 1024], P(('inner', 'outer', 'head'))
Inputs may be any that keep to these rules, and one draw needn't show every extreme that they name: Each aligned run of 128 rows holds 128 consecutive positions in increasing order; every position appears once. `doc_lengths`: the lengths sum to 7680; the largest is exactly 768.
All inputs are finite; a program needn't handle non-finite values.
Results may differ from a plain program's by a relative error of at most 0.03.
Values may be sent and summed in bfloat16 or wider, within the bound.
No kernel may reach another device: no remote copies, remote signals or barrier semaphores. Data moves between devices by JAX's collectives and lax.ppermute only.
A program may use at most 128 MiB of HBM per device.

v0:
```python
import jax
import jax.numpy as jnp
from jax import lax
from jax.sharding import PartitionSpec as P

HD = 128
GROUP = 4


negative = -1e30


def document_of(where_pos, ends):
    return jnp.sum((ends[None, :] <= where_pos[:, None]).astype(jnp.int32), axis=1)


def visible(query_pos, query_doc, key_pos, key_doc):
    return (key_doc[None, :] == query_doc[:, None]) & (key_pos[None, :] <= query_pos[:, None])


def block_size(count, shard):
    pieces = count // shard
    best = 1
    for factor in range(1, pieces + 1):
        if pieces % factor == 0 and factor * shard <= 1024:
            best = factor
    return best * shard


def per_device(queries, keys, values, grad_out, doc_lengths, positions):
    head_q, head_k, head_v, head_g = (
        lax.all_to_all(queries, "head", split_axis=1, concat_axis=0, tiled=True),
        lax.all_to_all(keys, "head", split_axis=1, concat_axis=0, tiled=True),
        lax.all_to_all(values, "head", split_axis=1, concat_axis=0, tiled=True),
        lax.all_to_all(grad_out, "head", split_axis=1, concat_axis=0, tiled=True),
    )
    rows = head_q.shape[0]
    width = HD
    group = GROUP
    scale = width ** (-0.5)
    ends = jnp.cumsum(doc_lengths)
    anchor = lax.axis_index(("inner", "outer")) * rows
    my_pos = lax.dynamic_slice_in_dim(positions, anchor, rows)
    my_doc = document_of(my_pos, ends)
    query3 = head_q.reshape(rows, group, width)
    grad3 = head_g.reshape(rows, group, width)
    seq_rows = positions.shape[0]

    def key_mask(start, count):
        key_pos = lax.dynamic_slice_in_dim(positions, start, count)
        return visible(my_pos, my_doc, key_pos, document_of(key_pos, ends))

    def tile_grads(query_b, grad_b, lse_b, delta_b, key_b, value_b, mask):
        mask3 = mask[:, None, :]
        scores = (
            jnp.einsum("rgd,kd->rgk", query_b, key_b, preferred_element_type=jnp.float32) * scale
        )
        prob = jnp.where(mask3, jnp.exp(scores - lse_b[..., None]), 0.0)
        dprob = jnp.einsum("rgd,kd->rgk", grad_b, value_b, preferred_element_type=jnp.float32)
        dscore = (prob * (dprob - delta_b[..., None])).astype(jnp.bfloat16)
        return (prob.astype(jnp.bfloat16), dscore)

    start_state = (
        jnp.zeros((rows, group, width), jnp.float32),
        jnp.full((rows, group), negative, jnp.float32),
        jnp.zeros((rows, group), jnp.float32),
    )
    piece = (
        lax.all_gather(head_k, ("inner", "outer"), axis=0, tiled=True),
        lax.all_gather(head_v, ("inner", "outer"), axis=0, tiled=True),
    )
    count_rows = piece[0].shape[0]
    block = block_size(count_rows, rows)
    number = count_rows // block
    key_blocks = piece[0].reshape(number, block, width)
    value_blocks = piece[1].reshape(number, block, width)

    def forward_visit(state, item):
        accum, top, norm = state
        key_b, value_b, index = item
        mask3 = key_mask(index * block, block)[:, None, :]
        scores = (
            jnp.einsum("rgd,kd->rgk", query3, key_b, preferred_element_type=jnp.float32) * scale
        )
        scores = jnp.where(mask3, scores, negative)
        new_top = jnp.maximum(top, jnp.max(scores, axis=2))
        factor = jnp.exp(top - new_top)
        weights = jnp.where(mask3, jnp.exp(scores - new_top[..., None]), 0.0)
        accum = accum * factor[..., None] + jnp.einsum(
            "rgk,kd->rgd", weights.astype(jnp.bfloat16), value_b, preferred_element_type=jnp.float32
        )
        norm = norm * factor + jnp.sum(weights, axis=2)
        return ((accum, new_top, norm), None)

    state, _ = lax.scan(
        forward_visit, start_state, (key_blocks, value_blocks, jnp.arange(number, dtype=jnp.int32))
    )
    accum, top, norm = state
    output = (accum / norm[..., None]).astype(jnp.bfloat16)
    log_total = top + jnp.log(norm)
    delta = jnp.sum(grad3.astype(jnp.float32) * output.astype(jnp.float32), axis=2)
    zero_q = jnp.zeros((rows, group, width), jnp.float32)
    zero_all = jnp.zeros((seq_rows, width), jnp.float32)
    initial = (zero_q, zero_all, zero_all)
    piece = (
        lax.all_gather(head_k, ("inner", "outer"), axis=0, tiled=True),
        lax.all_gather(head_v, ("inner", "outer"), axis=0, tiled=True),
    )
    count_rows = piece[0].shape[0]
    backward_block = block_size(count_rows, rows)
    number = count_rows // backward_block
    key_blocks = piece[0].reshape(number, backward_block, width)
    value_blocks = piece[1].reshape(number, backward_block, width)

    def backward_visit(state, item):
        grad_q, grad_k_all, grad_v_all = state
        key_b, value_b, index = item
        offset = index * backward_block
        mask = key_mask(offset, backward_block)
        prob_low, dscore = tile_grads(query3, grad3, log_total, delta, key_b, value_b, mask)
        grad_q = (
            grad_q
            + jnp.einsum("rgk,kd->rgd", dscore, key_b, preferred_element_type=jnp.float32) * scale
        )
        key_term = (
            jnp.einsum("rgk,rgd->kd", dscore, query3, preferred_element_type=jnp.float32) * scale
        )
        value_term = jnp.einsum("rgk,rgd->kd", prob_low, grad3, preferred_element_type=jnp.float32)
        grad_k_all = lax.dynamic_update_slice_in_dim(
            grad_k_all,
            lax.dynamic_slice_in_dim(grad_k_all, offset, backward_block, 0) + key_term,
            offset,
            0,
        )
        grad_v_all = lax.dynamic_update_slice_in_dim(
            grad_v_all,
            lax.dynamic_slice_in_dim(grad_v_all, offset, backward_block, 0) + value_term,
            offset,
            0,
        )
        return ((grad_q, grad_k_all, grad_v_all), None)

    state, _ = lax.scan(
        backward_visit, initial, (key_blocks, value_blocks, jnp.arange(number, dtype=jnp.int32))
    )
    grad_q, grad_k_all, grad_v_all = state
    grad_k, grad_v = (
        lax.psum_scatter(
            grad_k_all.astype(jnp.bfloat16), ("inner", "outer"), scatter_dimension=0, tiled=True
        ).astype(jnp.float32),
        lax.psum_scatter(
            grad_v_all.astype(jnp.bfloat16), ("inner", "outer"), scatter_dimension=0, tiled=True
        ).astype(jnp.float32),
    )
    results = (
        lax.all_to_all(
            output.reshape(rows, group * width), "head", split_axis=0, concat_axis=1, tiled=True
        ),
        lax.all_to_all(
            grad_q.astype(jnp.bfloat16).reshape(rows, group * width),
            "head",
            split_axis=0,
            concat_axis=1,
            tiled=True,
        ),
        lax.all_to_all(
            grad_k.astype(jnp.bfloat16), "head", split_axis=0, concat_axis=1, tiled=True
        ),
        lax.all_to_all(
            grad_v.astype(jnp.bfloat16), "head", split_axis=0, concat_axis=1, tiled=True
        ),
    )
    return (results[0], results[1], results[2], results[3])


def solution(mesh):
    return jax.shard_map(
        per_device,
        mesh=mesh,
        in_specs=(
            P(("inner", "outer", "head"), None),
            P(("inner", "outer", "head"), None),
            P(("inner", "outer", "head"), None),
            P(("inner", "outer", "head"), None),
            P(),
            P(),
        ),
        out_specs=(
            P(("inner", "outer", "head"), None),
            P(("inner", "outer", "head"), None),
            P(("inner", "outer", "head"), None),
            P(("inner", "outer", "head"), None),
        ),
        check_vma=False,
    )
```

profile of v0, /device:TPU:1, one launch (start us, length us, event | category | flops | bytes accessed | tf_op | source)
XLA Modules:
  0.0 909.2 jit_solution(16900254911646056234)
XLA Ops:
  8.1 17.1 %all_to_all.146 = bf16[30,8,128]{2,0,1:T(8,128)(2,1)S(1)} all-to-all(bf16[30,8,128]{2,0,1:T(8,128)(2,1)S(1)} %copy.68), channel_id=1, replica_groups=mesh['head'=8,'inner'=4,'outer'=8] {'head'}, dimensions={1} | all-to-all | bytes 122880 | tf_op jit(solution)/shard_map/all_to_all | solution.py:33
  26.8 10.7 %all_to_all.147 = bf16[30,8,128]{2,0,1:T(8,128)(2,1)S(1)} all-to-all(bf16[30,8,128]{2,0,1:T(8,128)(2,1)S(1)} %copy.70), channel_id=1, replica_groups=mesh['head'=8,'inner'=4,'outer'=8] {'head'}, dimensions={1} | all-to-all | bytes 122880 | tf_op jit(solution)/shard_map/all_to_all | solution.py:34
  40.0 4.4 all-to-all-start.1
  46.2 10.7 %all-to-all-done.1 = bf16[30,8,512]{2,0,1:T(8,128)(2,1)S(1)} async-done(((bf16[30,8,512]{2,0,1:T(8,128)(2,1)}), bf16[30,8,512]{2,0,1:T(8,128)(2,1)S(1)}, u32[]{:S(2)}, u32[]{:S(2)}) %all-to-all-start.1) | async-done | bytes 245792 | tf_op jit(solution)/shard_map/all_to_all | solution.py:32
  56.9 3.9 all-to-all-start.4
  62.1 11.8 %all-to-all-done.4 = bf16[30,8,512]{2,0,1:T(8,128)(2,1)S(1)} async-done(((bf16[30,8,512]{2,0,1:T(8,128)(2,1)}), bf16[30,8,512]{2,0,1:T(8,128)(2,1)S(1)}, u32[]{:S(2)}, u32[]{:S(2)}) %all-to-all-start.4) | async-done | bytes 245792 | tf_op jit(solution)/shard_map/all_to_all | solution.py:35
  74.0 85.5 %all-gather.3.cloned.1.call-done = bf16[7680,128]{1,0:T(8,128)(2,1)} async-done(((bf16[240,128]{1,0:T(8,128)(2,1)}), bf16[7680,128]{1,0:T(8,128)(2,1)}) %all-gather.3.cloned.1.call-update) | async-done | bytes 1966096 | tf_op jit(solution)/shard_map/all_gather | solution.py:69
  159.5 158.3 %all-gather.5.cloned.1.call-done = bf16[7680,128]{1,0:T(8,128)(2,1)} async-done(((bf16[240,128]{1,0:T(8,128)(2,1)}), bf16[7680,128]{1,0:T(8,128)(2,1)}) %all-gather.5.cloned.1.call-update) | async-done | bytes 1966096 | tf_op jit(solution)/shard_map/all_gather | solution.py:70
  317.8 96.6 %while.30 = (s32[]{:T(128)}, f32[240,4,128]{2,0,1:T(8,128)S(1)}, f32[240,4]{0,1:T(4,128)S(1)}, f32[240,4]{0,1:T(4,128)S(1)}, s32[16]{0:T(128)S(1)}, /*index=5*/s...) while((s32[]{:T(128)}, f32[240,4,128]{2,0,1:T(8,128)S(1)}, ...), condition=%wide.region_6.7_spmd.clone, body=%wide.region_2.6_spmd.clone.sunk | while | flops 484949760 | bytes 28534456 | solution.py:95
  320.3 3.7 fusion.84
  324.0 3.3 fusion.85
  327.3 2.6 fusion.87
  332.4 3.7 fusion.84
  336.1 3.3 fusion.85
  339.4 2.6 fusion.87
  344.5 3.7 fusion.84
  348.1 3.3 fusion.85
  351.5 2.6 fusion.87
  356.5 3.7 fusion.84
  360.2 3.3 fusion.85
  363.5 2.6 fusion.87
  368.6 3.7 fusion.84
  372.3 3.3 fusion.85
  375.6 2.6 fusion.87
  380.7 3.7 fusion.84
  384.4 3.3 fusion.85
  387.7 2.6 fusion.87
  392.8 3.7 fusion.84
  396.4 3.3 fusion.85
  399.8 2.6 fusion.87
  404.8 3.7 fusion.84
  408.5 3.3 fusion.85
  411.8 2.6 fusion.87
  419.6 111.6 %while.31 = (s32[]{:T(128)}, f32[240,4,128]{2,0,1:T(8,128)S(1)}, f32[7680,128]{1,0:T(8,128)}, f32[7680,128]{1,0:T(8,128)}, s32[16]{0:T(128)S(1)}, /*index=5*/s32...) while((s32[]{:T(128)}, f32[240,4,128]{2,0,1:T(8,128)S(1)}, ...), condition=%wide.region_10.11_spmd.clone, body=%wide.region_8.10_spmd.clone.sunk | while | flops 1190337536 | bytes 21987772 | solution.py:143
  423.7 2.3 fusion.99
  426.0 2.5 fusion.101
  428.6 3.2 fusion.102
  437.7 2.3 fusion.99
  440.0 2.6 fusion.101
  442.5 3.2 fusion.102
  451.6 2.3 fusion.99
  453.9 2.6 fusion.101
  456.5 3.2 fusion.102
  467.9 2.5 fusion.101
  470.4 3.2 fusion.102
  481.9 2.6 fusion.101
  484.4 3.2 fusion.102
  495.8 2.5 fusion.101
  498.4 3.2 fusion.102
  509.8 2.5 fusion.101
  512.3 3.2 fusion.102
  521.5 2.3 fusion.99
  523.8 2.5 fusion.101
  526.3 3.2 fusion.102
  531.3 3.7 convert_element_type.45
  535.1 3.6 convert_element_type.46
  539.6 27.5 %all-to-all-start.5 = ((bf16[8,30,512]{2,1,0:T(8,128)(2,1)}), bf16[8,30,512]{2,1,0:T(8,128)(2,1)S(1)}, u32[]{:S(2)}, u32[]{:S(2)}) async-start(bf16[8,30,512]{2,1,0:T(8,128)(2,1)} %all_to_all.126), calls=%async_computation.5 | async-start | bytes 524288 | tf_op jit(solution)/shard_map/all_to_all | solution.py:159
  567.9 9.0 all-to-all-done.5
  576.9 4.9 all-to-all-start.3
  581.8 115.9 %reduce-scatter.3.cloned.1.call-done = bf16[240,128]{1,0:T(8,128)(2,1)} async-done(((bf16[7680,128]{1,0:T(8,128)(2,1)}), bf16[240,128]{1,0:T(8,128)(2,1)}) %reduce-scatter.3.cloned.1.call-update) | async-done | bytes 61456 | tf_op jit(solution)/shard_map/reduce_scatter | solution.py:148
  699.1 31.5 %all-to-all-start.6 = ((bf16[8,30,128]{2,1,0:T(8,128)(2,1)}), bf16[8,30,128]{2,1,0:T(8,128)(2,1)S(1)}, u32[]{:S(2)}, u32[]{:S(2)}) async-start(bf16[8,30,128]{2,1,0:T(8,128)(2,1)} %all_to_all.130), calls=%async_computation.7 | async-start | bytes 131072 | tf_op jit(solution)/shard_map/all_to_all | solution.py:166
  730.6 131.2 %reduce-scatter.5.cloned.1.call-done = bf16[240,128]{1,0:T(8,128)(2,1)} async-done(((bf16[7680,128]{1,0:T(8,128)(2,1)}), bf16[240,128]{1,0:T(8,128)(2,1)}) %reduce-scatter.5.cloned.1.call-update) | async-done | bytes 61456 | tf_op jit(solution)/shard_map/reduce_scatter | solution.py:151
  863.2 31.3 %all-to-all-start.7 = ((bf16[8,30,128]{2,1,0:T(8,128)(2,1)}), bf16[8,30,128]{2,1,0:T(8,128)(2,1)S(1)}, u32[]{:S(2)}, u32[]{:S(2)}) async-start(bf16[8,30,128]{2,1,0:T(8,128)(2,1)} %all_to_all.134), calls=%async_computation.9 | async-start | bytes 131072 | tf_op jit(solution)/shard_map/all_to_all | solution.py:169
  897.1 4.8 all-to-all-done.7
  (189 shorter events, 86.9 us)
Async XLA Ops:
  7.2 53.7 %copy-start.1 = (s32[16]{0:T(128)S(1)}, s32[16]{0:T(128)}, u32[]{:S(2)}) copy-start(s32[16]{0:T(128)} %param.14) | copy-start | bytes 196
  7.2 152.3 %all-gather.3.cloned.1.call-start = ((), (), s32[]{:S(2)}) async-start(), calls=%async_computation.10 | async-start | bytes 2027520 | tf_op jit(solution)/shard_map/all_gather | solution.py:69
  25.9 292.0 %all-gather.5.cloned.1.call-start = ((), (), s32[]{:S(2)}) async-start(), calls=%async_computation.11 | async-start | bytes 2027520 | tf_op jit(solution)/shard_map/all_gather | solution.py:70
  40.0 16.9 %all-to-all-start.1 = ((bf16[30,8,512]{2,0,1:T(8,128)(2,1)}), bf16[30,8,512]{2,0,1:T(8,128)(2,1)S(1)}, u32[]{:S(2)}, u32[]{:S(2)}) async-start(bf16[30,8,512]{2,0,1:T(8,128)(2,1)} %copy.69), calls=%async_computation.1 | async-start | bytes 524288 | tf_op jit(solution)/shard_map/all_to_all | solution.py:32
  56.9 16.9 %all-to-all-start.4 = ((bf16[30,8,512]{2,0,1:T(8,128)(2,1)}), bf16[30,8,512]{2,0,1:T(8,128)(2,1)S(1)}, u32[]{:S(2)}, u32[]{:S(2)}) async-start(bf16[30,8,512]{2,0,1:T(8,128)(2,1)} %copy.75), calls=%async_computation.4 | async-start | bytes 524288 | tf_op jit(solution)/shard_map/all_to_all | solution.py:35
  60.8 636.8 %reduce-scatter.3.cloned.1.call-start = ((), (), s32[]{:S(2)}) async-start(), calls=%async_computation.12 | async-start | bytes 2027520 | tf_op jit(solution)/shard_map/reduce_scatter | solution.py:148
  324.0 3.3 copy-start
  336.0 3.3 copy-start
  348.1 3.3 copy-start
  360.2 3.3 copy-start
  372.3 3.3 copy-start
  384.4 3.3 copy-start
  396.4 3.3 copy-start
  408.5 3.3 copy-start
  535.0 326.8 %reduce-scatter.5.cloned.1.call-start = ((), (), s32[]{:S(2)}) async-start(), calls=%async_computation.13 | async-start | bytes 2027520 | tf_op jit(solution)/shard_map/reduce_scatter | solution.py:151
  539.6 37.2 %all-to-all-start.5 = ((bf16[8,30,512]{2,1,0:T(8,128)(2,1)}), bf16[8,30,512]{2,1,0:T(8,128)(2,1)S(1)}, u32[]{:S(2)}, u32[]{:S(2)}) async-start(bf16[8,30,512]{2,1,0:T(8,128)(2,1)} %all_to_all.126), calls=%async_computation.5 | async-start | bytes 524288 | tf_op jit(solution)/shard_map/all_to_all | solution.py:159
  576.9 122.3 %all-to-all-start.3 = ((bf16[8,30,512]{2,1,0:T(8,128)(2,1)}), bf16[8,30,512]{2,1,0:T(8,128)(2,1)S(1)}, u32[]{:S(2)}, u32[]{:S(2)}) async-start(bf16[8,30,512]{2,1,0:T(8,128)(2,1)} %all_to_all.119), calls=%async_computation.3 | async-start | bytes 524288 | tf_op jit(solution)/shard_map/all_to_all | solution.py:156
  699.1 164.1 %all-to-all-start.6 = ((bf16[8,30,128]{2,1,0:T(8,128)(2,1)}), bf16[8,30,128]{2,1,0:T(8,128)(2,1)S(1)}, u32[]{:S(2)}, u32[]{:S(2)}) async-start(bf16[8,30,128]{2,1,0:T(8,128)(2,1)} %all_to_all.130), calls=%async_computation.7 | async-start | bytes 131072 | tf_op jit(solution)/shard_map/all_to_all | solution.py:166
  863.2 38.7 %all-to-all-start.7 = ((bf16[8,30,128]{2,1,0:T(8,128)(2,1)}), bf16[8,30,128]{2,1,0:T(8,128)(2,1)S(1)}, u32[]{:S(2)}, u32[]{:S(2)}) async-start(bf16[8,30,128]{2,1,0:T(8,128)(2,1)} %all_to_all.134), calls=%async_computation.9 | async-start | bytes 131072 | tf_op jit(solution)/shard_map/all_to_all | solution.py:169
Sparse Core Ops, SparseCore 0:
  26.0 133.4 all-gather.2
  161.9 155.9 all-gather.4
  535.1 162.4 reduce-scatter.2
  700.2 161.5 reduce-scatter.4
where the time goes:
time: 913 us; the launch traced here: 909 us
  waiting for transfers between devices  527 us (58%)
  matrix products  142 us (16%)
  starting transfers between devices  104 us (11%)
  local copies, waits for them, and re-layouts  42 us (5%)
  other arithmetic  41.3 us (5%)
  blocking collectives  27.8 us (3%)
  between operations  14 us (2%)
  loops' own time  11.3 us (1%)
    all_gather x1, waiting for transfers between devices, per_device(): lax.all_gather(head_v, ('inner', 'outer'), axis=0, tiled=True)  158 us
    reduce_scatter x1, waiting for transfers between devices, per_device(): lax.psum_scatter(grad_v_all.astype(jnp.bfloat16), ('inner', 'outer'), sca...  131 us
    reduce_scatter x1, waiting for transfers between devices, per_device(): lax.psum_scatter(grad_k_all.astype(jnp.bfloat16), ('inner', 'outer'), sca...  116 us
    all_gather x1, waiting for transfers between devices, per_device(): lax.all_gather(head_k, ('inner', 'outer'), axis=0, tiled=True)  85.5 us
    all_to_all x1, starting transfers between devices, per_device(): lax.all_to_all(grad_k.astype(jnp.bfloat16), 'head', split_axis=0, concat_...  31.5 us
    all_to_all x1, starting transfers between devices, per_device(): lax.all_to_all(grad_v.astype(jnp.bfloat16), 'head', split_axis=0, concat_...  31.3 us
    dot_general x8, matrix products, forward_visit(): jnp.einsum('rgd,kd->rgk', query3, key_b, preferred_element_type=jnp.float32)  29.3 us
    all_to_all x1, starting transfers between devices, per_device(): lax.all_to_all(grad_q.astype(jnp.bfloat16).reshape(rows, group * width),...  27.5 us
  transfers between devices with their start and end apart: 10, of which 8 were waited for; matrix products, arithmetic and copies ran while one was open for 1% of the time, Pallas kernels for 0%

commit v1 on v0

v1 whole, which is shorter than its diff:
```python
import jax
import jax.numpy as jnp
from jax import lax
from jax.experimental import pallas as pl
from jax.experimental.pallas import tpu as pltpu
from jax.sharding import PartitionSpec as P

HD = 128
GROUP = 4
KVH = 8
RUN = 128
BACK = 3
SPREAD = 32
BLOCK = 256
UNIT = 10
LOCAL = 30
SCALE = HD**-0.5
LOG2E = 1.4426950408889634
NEGATIVE = -1e30
ALL = ("head", "inner", "outer")
SEQ_AXES = ("inner", "outer")
LIMIT = 48 * 1024 * 1024

f32, bf16, i32 = jnp.float32, jnp.bfloat16, jnp.int32


def iota(shape, dim):
    return lax.broadcasted_iota(i32, shape, dim)


def one_hot(condition):
    return jnp.where(condition, 1.0, 0.0).astype(bf16)


def dot(a, b):
    return jnp.dot(a, b, preferred_element_type=f32)


def dot_nt(a, b):
    return lax.dot_general(a, b, (((1,), (1,)), ((), ())), preferred_element_type=f32)


def first_row():
    device = lax.axis_index("inner") * 64 + lax.axis_index("outer") * 8 + lax.axis_index("head")
    return (device * LOCAL) & (SPREAD - 1)


def seq_index():
    return lax.axis_index("inner") * 8 + lax.axis_index("outer")


def spread_row(packed, shift):
    token = packed & 31
    to = ((shift + token) & 31) * UNIT + (packed >> 5)
    return jnp.where(token < LOCAL, to, -1)


def place_spread(rows_are_units):
    size = UNIT * 32
    to = spread_row(iota((size, size), int(rows_are_units)), first_row())
    return one_hot(iota((size, size), 1 - int(rows_are_units)) == to)


def pack_kernel(q_ref, k_ref, v_ref, g_ref, out_ref, qs, ks, vs, gs, x_ref, o_ref, in_sem, out_sem):
    size = UNIT * 32
    wide, pairs = 2 * GROUP * HD, KVH // 2
    arrivals = []
    for i, (source, to) in enumerate(((k_ref, ks), (v_ref, vs))):
        arrivals.append(pltpu.make_async_copy(source, to, in_sem.at[i]))
    for pair in range(pairs):
        at = pl.ds(pair * wide, wide)
        for i, (source, to) in enumerate(((q_ref, qs), (g_ref, gs))):
            arrivals.append(
                pltpu.make_async_copy(source.at[:, at], to.at[:, at], in_sem.at[2 + 2 * pair + i])
            )
    for copy in arrivals:
        copy.start()
    x_ref[...] = jnp.zeros_like(x_ref)
    place = place_spread(True)
    departures = []
    for pair in range(pairs):
        for copy in arrivals[2 * pair + 2 : 2 * pair + 4] + (arrivals[:2] if pair == 0 else []):
            copy.wait()
        for head in (2 * pair, 2 * pair + 1):
            to = pl.ds(head * HD, HD)
            for g in range(GROUP):
                column = pl.ds((head * GROUP + g) * HD, HD)
                x_ref[pl.ds(g * 32, LOCAL), to] = qs[:, column]
                x_ref[pl.ds((GROUP + g) * 32, LOCAL), to] = gs[:, column]
            x_ref[pl.ds(8 * 32, LOCAL), to] = ks[:, to]
            x_ref[pl.ds(9 * 32, LOCAL), to] = vs[:, to]
        rows = dot(place, x_ref[:, pl.ds(pair * 2 * HD, 2 * HD)]).astype(bf16)
        o_ref[pl.ds(2 * pair * size, size), :] = rows[:, :HD]
        o_ref[pl.ds((2 * pair + 1) * size, size), :] = rows[:, HD:]
        at = pl.ds(2 * pair * size, 2 * size)
        departures.append(pltpu.make_async_copy(o_ref.at[at, :], out_ref.at[at, :], out_sem.at[pair]))
        departures[-1].start()
    for copy in departures:
        copy.wait()


def unpack_kernel(r_ref, place_ref, att_ref, gq_ref, gk_ref, gv_ref, qs, ks, vs, gs, x_ref, sem):
    size = UNIT * 32
    wide, pairs = 2 * GROUP * HD, KVH // 2
    departures = []
    for pair in range(pairs):
        for half in range(2):
            x_ref[pair, :, pl.ds(half * HD, HD)] = r_ref[pl.ds((2 * pair + half) * size, size), :]
        rows = dot(place_ref[...], x_ref[pair]).astype(bf16)
        for half in range(2):
            head = 2 * pair + half
            part = rows[:, half * HD : (half + 1) * HD]
            to = pl.ds(head * HD, HD)
            for g in range(GROUP):
                column = pl.ds((head * GROUP + g) * HD, HD)
                qs[:, column] = part[g * 32 : g * 32 + LOCAL]
                gs[:, column] = part[(GROUP + g) * 32 : (GROUP + g) * 32 + LOCAL]
            ks[:, to] = part[8 * 32 : 8 * 32 + LOCAL]
            vs[:, to] = part[9 * 32 : 9 * 32 + LOCAL]
        at = pl.ds(pair * wide, wide)
        for source, to in ((qs, att_ref), (gs, gq_ref)):
            departures.append(
                pltpu.make_async_copy(source.at[:, at], to.at[:, at], sem.at[len(departures)])
            )
            departures[-1].start()
    for source, to in ((ks, gk_ref), (vs, gv_ref)):
        departures.append(pltpu.make_async_copy(source, to, sem.at[len(departures)]))
        departures[-1].start()
    for copy in departures:
        copy.wait()


def sender(run, slot, group):
    row = run * RUN + (slot & 3) * 32 + group
    device = (row * 34953) >> 20
    return jnp.where(run >= 0, ((device & 7) << 5) + (device >> 3), -1)


def position(row):
    return ((row >> 2) & 1) * RUN + (row & 3) * 32 + (row >> 3)


def table_kernel(
    run_row_ref, run_col_ref, lengths_ref, sort_ref, unsort_ref, unpack_ref, begin_ref
):
    group = seq_index()
    query_pos = group * BLOCK + position(iota((1, BLOCK), 1))
    begin = jnp.zeros((1, BLOCK), i32)
    end = jnp.int32(0)
    for i in range(16):
        end = end + lengths_ref[i]
        begin = jnp.where(query_pos >= end, end, begin)
    begin_ref[...] = begin
    number = iota((BLOCK, 64), 1)
    for b in range(BACK + 1):
        slot = iota((BLOCK, 1), 0)
        found = run_row_ref[...] == (slot >> 2) - 2 * b
        run = jnp.max(jnp.where(found, number, -1), axis=1, keepdims=True)
        sort_ref[pl.ds(b * BLOCK, BLOCK), :] = one_hot(
            iota((BLOCK, BLOCK), 1) == sender(run, slot, group)
        )
    slot = iota((1, BLOCK), 1)
    found = run_col_ref[...] == (slot >> 2)
    run = jnp.max(jnp.where(found, iota((64, BLOCK), 0), -1), axis=0, keepdims=True)
    unsort_ref[...] = one_hot(iota((BLOCK, BLOCK), 0) == sender(run, slot, group))
    unpack_ref[...] = place_spread(False)


def sort_kernel(r_ref, place_ref, out_ref, wide_ref, x_ref):
    wide_ref[...] = r_ref[...].astype(f32)
    for u in range(UNIT):
        x_ref[:, pl.ds(u * HD, HD)] = wide_ref[pl.ds(u, BLOCK, stride=UNIT), :].astype(bf16)
    out_ref[:, pl.ds(0, 1280)] = dot(place_ref[pl.ds(0, BLOCK), :], x_ref[...]).astype(bf16)
    for b in range(1, BACK + 1):
        out_ref[:, pl.ds(1024 + 256 * b, 256)] = dot(
            place_ref[pl.ds(b * BLOCK, BLOCK), :], x_ref[:, pl.ds(1024, 256)]
        ).astype(bf16)


def unsort_kernel(r_ref, place_ref, out_ref, wide_ref, sum_ref, x_ref):
    for b in range(BACK + 1):
        part = r_ref[b:SPREAD, :, pl.ds(1024 + 256 * b, 256)].astype(f32)
        part = part.reshape((SPREAD - b) * 8, 256)
        rows = pl.ds(0, (SPREAD - b) * 8)
        if b == 0:
            sum_ref[rows, :] = part
        else:
            sum_ref[rows, :] = sum_ref[rows, :] + part
    x_ref[:, pl.ds(0, 1024)] = r_ref[:, :, pl.ds(0, 1024)].reshape(BLOCK, 1024)
    x_ref[:, pl.ds(1024, 256)] = sum_ref[...].astype(bf16)
    for pair in range(UNIT // 2):
        rows = dot(place_ref[...], x_ref[:, pl.ds(pair * 2 * HD, 2 * HD)])
        wide_ref[pl.ds(2 * pair, BLOCK, stride=UNIT), :] = rows[:, :HD]
        wide_ref[pl.ds(2 * pair + 1, BLOCK, stride=UNIT), :] = rows[:, HD:]
    out_ref[...] = wide_ref[...].astype(bf16)


def attention_kernel(
    begin_ref, m_ref, to_ref, out_ref, bias_ref, s_ref, dp_ref, p_ref, d_ref, q_ref, g_ref, k_ref,
    v_ref, sem,
):
    base = seq_index() * BLOCK
    blocks, heads = range(BACK + 1), range(GROUP)

    def rows(b):
        return pl.ds(b * BLOCK, BLOCK)

    departures = []

    def send(first, count):
        at = pl.ds(first, count)
        departures.append(
            pltpu.make_async_copy(out_ref.at[:, at], to_ref.at[:, at], sem.at[len(departures)])
        )
        departures[-1].start()

    query_pos = base + position(iota((1, BLOCK), 1))
    begin = begin_ref[...]
    key_pos = base + position(iota((BLOCK, BLOCK), 0))
    for b in blocks:
        seen = key_pos >= begin + b * BLOCK
        if b == 0:
            seen = seen & (key_pos <= query_pos)
        bias_ref[rows(b), :] = jnp.where(seen, 0.0, NEGATIVE)
        k_ref[rows(b), :] = m_ref[:, pl.ds(1024 + 256 * b, HD)]
        v_ref[rows(b), :] = m_ref[:, pl.ds(1024 + 256 * b + HD, HD)]
    for g in heads:
        q_ref[rows(g), :] = m_ref[:, pl.ds(g * HD, HD)]
        g_ref[rows(g), :] = m_ref[:, pl.ds((GROUP + g) * HD, HD)]
    keys, values = k_ref[...], v_ref[...]
    keys_t, values_t = keys.T, values.T

    tops, inverses, deltas = [], [], []
    for g in heads:
        s = dot_nt(keys, q_ref[rows(g), :]) * (SCALE * LOG2E) + bias_ref[...]
        s_ref[:, rows(g)] = s
        tops.append(jnp.max(s, axis=0, keepdims=True))
        dp_ref[:, rows(g)] = dot_nt(values, g_ref[rows(g), :])
    for g in heads:
        weights = jnp.exp2(s_ref[:, rows(g)] - tops[g])
        s_ref[:, rows(g)] = weights
        inverse = 1.0 / jnp.sum(weights, axis=0, keepdims=True)
        output = (dot(values_t, weights.astype(bf16)) * inverse).T.astype(bf16)
        out_ref[:, pl.ds(g * HD, HD)] = output
        product = g_ref[rows(g), :].astype(f32) * output.astype(f32)
        deltas.append(jnp.sum(product.T, axis=0, keepdims=True))
        inverses.append(inverse)
    send(0, GROUP * HD)
    for g in heads:
        prob = s_ref[:, rows(g)] * inverses[g]
        p_ref[:, rows(g)] = prob.astype(bf16)
        dscore = (prob * (dp_ref[:, rows(g)] - deltas[g])).astype(bf16)
        d_ref[:, rows(g)] = dscore
        out_ref[:, pl.ds((GROUP + g) * HD, HD)] = (dot(keys_t, dscore) * SCALE).T.astype(bf16)
    send(GROUP * HD, GROUP * HD)
    for b in blocks:
        at = 2 * GROUP * HD + 2 * HD * b
        out_ref[:, pl.ds(at, HD)] = (dot(d_ref[rows(b), :], q_ref[...]) * SCALE).astype(bf16)
        out_ref[:, pl.ds(at + HD, HD)] = dot(p_ref[rows(b), :], g_ref[...]).astype(bf16)
        send(at, 2 * HD)
    for copy in departures:
        copy.wait()


VMEM = pl.BlockSpec(memory_space=pltpu.VMEM)
ANY = pl.BlockSpec(memory_space=pl.ANY)


def call(kernel, outs, scratch, *args, place_in=VMEM, place_out=VMEM, limit=LIMIT):
    return pl.pallas_call(
        kernel,
        out_shape=[jax.ShapeDtypeStruct(o, bf16) for o in outs],
        in_specs=[place_in] * len(args),
        out_specs=[place_out] * len(outs),
        scratch_shapes=scratch,
        compiler_params=pltpu.CompilerParams(vmem_limit_bytes=limit),
    )(*args)


def exchange(x, axes):
    return lax.all_to_all(x, axes, split_axis=0, concat_axis=0, tiled=True)


def per_device(queries, keys, values, grad_out, doc_lengths, positions):
    units, size = 256 * UNIT, UNIT * 32
    wide, narrow = (LOCAL, KVH * GROUP * HD), (LOCAL, KVH * HD)
    local = [pltpu.VMEM(s, bf16) for s in (wide, narrow, narrow, wide)]
    runs = jnp.pad(positions[::RUN] // RUN, (0, 4), constant_values=-1000)
    table = pl.pallas_call(
        table_kernel,
        out_shape=[
            jax.ShapeDtypeStruct(((BACK + 1) * BLOCK, BLOCK), bf16),
            jax.ShapeDtypeStruct((BLOCK, BLOCK), bf16),
            jax.ShapeDtypeStruct((size, size), bf16),
            jax.ShapeDtypeStruct((1, BLOCK), i32),
        ],
        in_specs=[VMEM, VMEM, pl.BlockSpec(memory_space=pltpu.SMEM)],
        out_specs=[VMEM] * 4,
        compiler_params=pltpu.CompilerParams(vmem_limit_bytes=LIMIT),
        cost_estimate=pl.CostEstimate(flops=1 << 24, bytes_accessed=1 << 18, transcendentals=0),
    )
    place_sort, place_unsort, place_unpack, begin = table(
        runs.reshape(1, 64), runs.reshape(64, 1), doc_lengths
    )
    (packed,) = call(
        pack_kernel,
        [(units, HD)],
        local
        + [
            pltpu.VMEM((size, KVH * HD), bf16),
            pltpu.VMEM((units, HD), bf16),
            pltpu.SemaphoreType.DMA((10,)),
            pltpu.SemaphoreType.DMA((4,)),
        ],
        queries,
        keys,
        values,
        grad_out,
        place_in=ANY,
        limit=None,
        place_out=ANY,
    )
    spread = exchange(packed.reshape(256, UNIT // 2, 2, HD), ALL).reshape(units, HD)
    (ordered,) = call(
        sort_kernel,
        [(BLOCK, 2048)],
        [pltpu.VMEM((units, HD), f32), pltpu.VMEM((BLOCK, 1280), bf16)],
        spread,
        place_sort,
    )
    block = exchange(ordered.reshape(SPREAD, 8, 2048), SEQ_AXES).reshape(BLOCK, 2048)
    square = (GROUP * BLOCK, (BACK + 1) * BLOCK)
    (done,) = call(
        attention_kernel,
        [(BLOCK, 2048)],
        [
            pltpu.VMEM((BLOCK, 2048), bf16),
            pltpu.VMEM((square[1], BLOCK), f32),
            pltpu.VMEM(square, f32),
            pltpu.VMEM(square, f32),
            pltpu.VMEM(square, bf16),
            pltpu.VMEM(square, bf16),
        ]
        + [pltpu.VMEM((square[0], HD), bf16)] * 4
        + [pltpu.SemaphoreType.DMA((6,))],
        begin,
        block,
        place_out=ANY,
    )
    back = exchange(done.reshape(SPREAD, 8, 2048), SEQ_AXES)
    (unsorted,) = call(
        unsort_kernel,
        [(units, HD)],
        [
            pltpu.VMEM((units, HD), f32),
            pltpu.VMEM((BLOCK, 256), f32),
            pltpu.VMEM((BLOCK, 1280), bf16),
        ],
        back,
        place_unsort,
    )
    home = exchange(unsorted.reshape(256, UNIT // 2, 2, HD), ALL).reshape(units, HD)
    return tuple(
        call(
            unpack_kernel,
            [wide, wide, narrow, narrow],
            local + [pltpu.VMEM((4, size, 2 * HD), bf16), pltpu.SemaphoreType.DMA((10,))],
            home,
            place_unpack,
            place_out=ANY,
        )
    )


def solution(mesh):
    rows = P(("inner", "outer", "head"), None)
    return jax.shard_map(
        per_device,
        mesh=mesh,
        in_specs=(rows, rows, rows, rows, P(), P()),
        out_specs=(rows, rows, rows, rows),
        check_vma=False,
    )
```

time: 913 us -> 122 us (0.13)
  waiting for transfers between devices: 527 us -> 19.6 us
  matrix products: 142 us -> 0 us
  starting transfers between devices: 104 us -> 15.7 us
  blocking collectives: 27.8 us -> 72 us
  other arithmetic: 41.3 us -> 0.01 us
  local copies, waits for them, and re-layouts: 42 us -> 1.65 us
  between operations: 14 us -> 0.69 us
  Pallas kernels: 0 us -> 12 us
  loops' own time: 11.3 us -> 0 us
    reduce_scatter x2 -> x0, waiting for transfers between devices: 247 us -> none  [the longest x1 131 us: per_device(): lax.psum_scatter(grad_v_all.astype(jnp.bfloat16), ('inner', 'outer'), sca...]
    all_gather x2 -> x0, waiting for transfers between devices: 244 us -> none  [the longest x1 158 us: per_device(): lax.all_gather(head_v, ('inner', 'outer'), axis=0, tiled=True)]
    dot_general x56 -> x0, matrix products: 142 us -> none  [the longest x8 29.3 us: forward_visit(): jnp.einsum('rgd,kd->rgk', query3, key_b, preferred_element_type=jnp.float32)]
    all_to_all x6 -> x1, starting transfers between devices: 103 us -> 15.7 us  [exchange(): return lax.all_to_all(x, axes, split_axis=0, concat_axis=0, tiled=True)]
    all_to_all x2 -> x3, blocking collectives: 27.8 us -> 72 us  [exchange(): return lax.all_to_all(x, axes, split_axis=0, concat_axis=0, tiled=True)]
    reduce_sum x26 -> x0, other arithmetic: 28.5 us -> none  [the longest x8 26.4 us: forward_visit(): norm = norm * factor + jnp.sum(weights, axis=2)]
    dynamic_slice x33 -> x0, local copies, waits for them, and re-layouts: 22.6 us -> none  [the longest x16 12.4 us: key_mask(): key_pos = lax.dynamic_slice_in_dim(positions, start, count)]
    all_to_all x6 -> x1, waiting for transfers between devices: 36.2 us -> 19.6 us  [exchange(): return lax.all_to_all(x, axes, split_axis=0, concat_axis=0, tiled=True)]
  transfers between devices with their start and end apart: 10 -> 1, of which waited for: 8 -> 1; matrix products, arithmetic and copies ran while one was open for 1% -> 1% of each run, Pallas kernels for 0% -> 1%
where the time goes in v1:
time: 122 us
  blocking collectives  72 us (59%)
  waiting for transfers between devices  19.6 us (16%)
  starting transfers between devices  15.7 us (13%)
  Pallas kernels  12 us (10%)
  local copies, waits for them, and re-layouts  1.65 us (1%)
    all_to_all x3, blocking collectives, exchange(): return lax.all_to_all(x, axes, split_axis=0, concat_axis=0, tiled=True)  72 us
    all_to_all x1, waiting for transfers between devices, exchange(): return lax.all_to_all(x, axes, split_axis=0, concat_axis=0, tiled=True)  19.6 us
    all_to_all x1, starting transfers between devices, exchange(): return lax.all_to_all(x, axes, split_axis=0, concat_axis=0, tiled=True)  15.7 us
    pallas_call x5, Pallas kernels, call(): pl.pallas_call(kernel, out_shape=[jax.ShapeDtypeStruct(o, bf16) for o in...  10.7 us
  transfers between devices with their start and end apart: 1, of which 1 were waited for; matrix products, arithmetic and copies ran while one was open for 1% of the time, Pallas kernels for 1%

profile of v1, /device:TPU:1, one launch (start us, length us, event | category | flops | bytes accessed | tf_op | source)
XLA Modules:
  0.0 121.6 jit_solution(375871079219993332)
XLA Ops:
  0.6 3.1 %shard_map.94 = bf16[2560,128]{1,0:T(8,128)(2,1)} custom-call(bf16[30,4096]{1,0:T(8,128)(2,1)} %q_ref.1, bf16[30,1024]{1,0:T(8,128)(2,1)} %k_ref.1, bf16[30,1024]{1,0:T(8,128)(2,1)} %v_ref.1, bf16[30,4096]{1,0:T(8,128)(2,1)} %g_ref.1), custom_call_target="tpu_custom_call" | custom-call | tf_op jit(solution)/shard_map/pallas_call | solution.py:270
  3.7 15.7 %all-to-all-start = ((bf16[256,5,2,128]{3,2,1,0:T(2,128)(2,1)}), bf16[256,5,2,128]{3,2,1,0:T(2,128)(2,1)S(1)}, u32[]{:S(2)}, u32[]{:S(2)}) async-start(bf16[256,5,2,128]{3,2,1,0:T(2,128)(2,1)} %bitcast.17), calls=%async_computation | async-start | bytes 1310720 | tf_op jit(solution)/shard_map/all_to_all | solution.py:281
  19.4 0.9 slice.3
  20.3 0.1 copy.10.run_col_ref
  20.4 0.0 copy-start
  20.4 0.7 copy-done
  21.0 1.3 %shard_map.93 = (bf16[1024,256]{1,0:T(8,128)(2,1)S(1)}, bf16[256,256]{1,0:T(8,128)(2,1)S(1)}, bf16[320,320]{1,0:T(8,128)(2,1)S(1)}, s32[1,256]{1,0:T(1,128)S(1)}) custom-call(s32[1,64]{1,0:T(1,128)S(1)} %get-tuple-element.13.run_row_ref, s32[64,1]{1,0:T(8,128)S(1)} %copy.10.run_col_ref, s32[16]{0:T(128)S(1)} %copy-done), custom_call_target="tpu_custom_call" | custom-call | flops 16777216 | bytes 262144 | tf_op jit(solution)/shard_map/pallas_call | solution.py:302
  22.4 19.6 %all-to-all-done = bf16[256,5,2,128]{3,2,1,0:T(2,128)(2,1)S(1)} async-done(((bf16[256,5,2,128]{3,2,1,0:T(2,128)(2,1)}), bf16[256,5,2,128]{3,2,1,0:T(2,128)(2,1)S(1)}, u32[]{:S(2)}, u32[]{:S(2)}) %all-to-all-start) | async-done | bytes 655392 | tf_op jit(solution)/shard_map/all_to_all | solution.py:281
  42.0 0.6 shard_map.95
  42.6 19.8 %all_to_all.20 = bf16[32,8,2048]{2,1,0:T(8,128)(2,1)S(1)} all-to-all(bf16[32,8,2048]{2,1,0:T(8,128)(2,1)S(1)} %bitcast.11), channel_id=1, replica_groups=mesh['head'=8,'inner'=4,'outer'=8] {'inner','outer'}, dimensions={0} | all-to-all | bytes 2097152 | tf_op jit(solution)/shard_map/all_to_all | solution.py:281
  62.4 5.3 %shard_map.96 = bf16[256,2048]{1,0:T(8,128)(2,1)S(1)} custom-call(s32[1,256]{1,0:T(1,128)S(1)} %get-tuple-element.8.begin_ref, bf16[256,2048]{1,0:T(8,128)(2,1)S(1)} %bitcast.12), custom_call_target="tpu_custom_call" | custom-call | tf_op jit(solution)/shard_map/pallas_call | solution.py:270
  67.7 21.1 %all_to_all.21.r_ref = bf16[32,8,2048]{2,1,0:T(8,128)(2,1)S(1)} all-to-all(bf16[32,8,2048]{2,1,0:T(8,128)(2,1)S(1)} %bitcast.13), channel_id=1, replica_groups=mesh['head'=8,'inner'=4,'outer'=8] {'inner','outer'}, dimensions={0} | all-to-all | bytes 2097152 | tf_op jit(solution)/shard_map/all_to_all | solution.py:281
  88.8 0.4 shard_map.97
  89.2 31.1 %all_to_all.22 = bf16[256,5,2,128]{3,2,1,0:T(2,128)(2,1)S(1)} all-to-all(bf16[256,5,2,128]{3,2,1,0:T(2,128)(2,1)S(1)} %bitcast.14), channel_id=1, replica_groups=mesh['head'=8,'inner'=4,'outer'=8] {'head','inner','outer'}, dimensions={0} | all-to-all | bytes 1310720 | tf_op jit(solution)/shard_map/all_to_all | solution.py:281
  120.3 1.3 %shard_map.98 = (bf16[30,4096]{1,0:T(8,128)(2,1)}, bf16[30,4096]{1,0:T(8,128)(2,1)}, bf16[30,1024]{1,0:T(8,128)(2,1)}, bf16[30,1024]{1,0:T(8,128)(2,1)}) custom-call(bf16[2560,128]{1,0:T(8,128)(2,1)S(1)} %bitcast.15, bf16[320,320]{1,0:T(8,128)(2,1)S(1)} %get-tuple-element.11.place_ref), custom_call_target="tpu_custom_call" | custom-call | tf_op jit(solution)/shard_map/pallas_call | solution.py:270
  (2 shorter events, 0.0 us)
Async XLA Ops:
  3.7 38.3 %all-to-all-start = ((bf16[256,5,2,128]{3,2,1,0:T(2,128)(2,1)}), bf16[256,5,2,128]{3,2,1,0:T(2,128)(2,1)S(1)}, u32[]{:S(2)}, u32[]{:S(2)}) async-start(bf16[256,5,2,128]{3,2,1,0:T(2,128)(2,1)} %bitcast.17), calls=%async_computation | async-start | bytes 1310720 | tf_op jit(solution)/shard_map/all_to_all | solution.py:281
  20.4 0.7 copy-start

commit v2 on v1

--- a/solution.py
+++ b/solution.py
@@ -3,6 +3,7 @@
 from jax import lax
 from jax.experimental import pallas as pl
 from jax.experimental.pallas import tpu as pltpu
+from jax.sharding import Mesh
 from jax.sharding import PartitionSpec as P
 
 HD = 128
@@ -17,8 +18,9 @@
 SCALE = HD**-0.5
 LOG2E = 1.4426950408889634
 NEGATIVE = -1e30
-ALL = ("head", "inner", "outer")
-SEQ_AXES = ("inner", "outer")
+ROWS = ("y", "z_lo", "x", "z_hi", "core")
+ALL = ("z_hi", "z_lo", "y", "x", "core")
+SEQ_AXES = ("y", "x", "core")
 LIMIT = 48 * 1024 * 1024
 
 f32, bf16, i32 = jnp.float32, jnp.bfloat16, jnp.int32
@@ -41,12 +43,14 @@
 
 
 def first_row():
-    device = lax.axis_index("inner") * 64 + lax.axis_index("outer") * 8 + lax.axis_index("head")
+    device = 0
+    for axis, size in zip(ROWS, (4, 2, 4, 4, 2)):
+        device = device * size + lax.axis_index(axis)
     return (device * LOCAL) & (SPREAD - 1)
 
 
 def seq_index():
-    return lax.axis_index("inner") * 8 + lax.axis_index("outer")
+    return lax.axis_index("y") * 8 + lax.axis_index("x") * 2 + lax.axis_index("core")
 
 
 def spread_row(packed, shift):
@@ -63,24 +67,18 @@
 
 def pack_kernel(q_ref, k_ref, v_ref, g_ref, out_ref, qs, ks, vs, gs, x_ref, o_ref, in_sem, out_sem):
     size = UNIT * 32
-    wide, pairs = 2 * GROUP * HD, KVH // 2
+    pairs = KVH // 2
     arrivals = []
-    for i, (source, to) in enumerate(((k_ref, ks), (v_ref, vs))):
+    for i, (source, to) in enumerate(((q_ref, qs), (g_ref, gs), (k_ref, ks), (v_ref, vs))):
         arrivals.append(pltpu.make_async_copy(source, to, in_sem.at[i]))
-    for pair in range(pairs):
-        at = pl.ds(pair * wide, wide)
-        for i, (source, to) in enumerate(((q_ref, qs), (g_ref, gs))):
-            arrivals.append(
-                pltpu.make_async_copy(source.at[:, at], to.at[:, at], in_sem.at[2 + 2 * pair + i])
-            )
+        arrivals[-1].start()
+    for u in range(UNIT):
+        x_ref[pl.ds(u * 32 + 16, 16), :] = jnp.zeros((16, KVH * HD), bf16)
+    place = place_spread(True)
     for copy in arrivals:
-        copy.start()
-    x_ref[...] = jnp.zeros_like(x_ref)
-    place = place_spread(True)
+        copy.wait()
     departures = []
     for pair in range(pairs):
-        for copy in arrivals[2 * pair + 2 : 2 * pair + 4] + (arrivals[:2] if pair == 0 else []):
-            copy.wait()
         for head in (2 * pair, 2 * pair + 1):
             to = pl.ds(head * HD, HD)
             for g in range(GROUP):
@@ -133,7 +131,9 @@
 def sender(run, slot, group):
     row = run * RUN + (slot & 3) * 32 + group
     device = (row * 34953) >> 20
-    return jnp.where(run >= 0, ((device & 7) << 5) + (device >> 3), -1)
+    y, z_lo, x = device >> 6, (device >> 5) & 1, (device >> 3) & 3
+    z_hi, core = (device >> 1) & 3, device & 1
+    return jnp.where(run >= 0, z_hi * 64 + z_lo * 32 + y * 8 + x * 2 + core, -1)
 
 
 def position(row):
@@ -196,23 +196,13 @@
 
 
 def attention_kernel(
-    begin_ref, m_ref, to_ref, out_ref, bias_ref, s_ref, dp_ref, p_ref, d_ref, q_ref, g_ref, k_ref,
-    v_ref, sem,
+    begin_ref, m_ref, out_ref, bias_ref, s_ref, dp_ref, p_ref, d_ref, q_ref, g_ref, k_ref, v_ref,
 ):
     base = seq_index() * BLOCK
     blocks, heads = range(BACK + 1), range(GROUP)
 
     def rows(b):
         return pl.ds(b * BLOCK, BLOCK)
-
-    departures = []
-
-    def send(first, count):
-        at = pl.ds(first, count)
-        departures.append(
-            pltpu.make_async_copy(out_ref.at[:, at], to_ref.at[:, at], sem.at[len(departures)])
-        )
-        departures[-1].start()
 
     query_pos = base + position(iota((1, BLOCK), 1))
     begin = begin_ref[...]
@@ -245,21 +235,16 @@
         product = g_ref[rows(g), :].astype(f32) * output.astype(f32)
         deltas.append(jnp.sum(product.T, axis=0, keepdims=True))
         inverses.append(inverse)
-    send(0, GROUP * HD)
     for g in heads:
         prob = s_ref[:, rows(g)] * inverses[g]
         p_ref[:, rows(g)] = prob.astype(bf16)
         dscore = (prob * (dp_ref[:, rows(g)] - deltas[g])).astype(bf16)
         d_ref[:, rows(g)] = dscore
         out_ref[:, pl.ds((GROUP + g) * HD, HD)] = (dot(keys_t, dscore) * SCALE).T.astype(bf16)
-    send(GROUP * HD, GROUP * HD)
     for b in blocks:
         at = 2 * GROUP * HD + 2 * HD * b
         out_ref[:, pl.ds(at, HD)] = (dot(d_ref[rows(b), :], q_ref[...]) * SCALE).astype(bf16)
         out_ref[:, pl.ds(at + HD, HD)] = dot(p_ref[rows(b), :], g_ref[...]).astype(bf16)
-        send(at, 2 * HD)
-    for copy in departures:
-        copy.wait()
 
 
 VMEM = pl.BlockSpec(memory_space=pltpu.VMEM)
@@ -309,7 +294,7 @@
         + [
             pltpu.VMEM((size, KVH * HD), bf16),
             pltpu.VMEM((units, HD), bf16),
-            pltpu.SemaphoreType.DMA((10,)),
+            pltpu.SemaphoreType.DMA((4,)),
             pltpu.SemaphoreType.DMA((4,)),
         ],
         queries,
@@ -334,18 +319,15 @@
         attention_kernel,
         [(BLOCK, 2048)],
         [
-            pltpu.VMEM((BLOCK, 2048), bf16),
             pltpu.VMEM((square[1], BLOCK), f32),
             pltpu.VMEM(square, f32),
             pltpu.VMEM(square, f32),
             pltpu.VMEM(square, bf16),
             pltpu.VMEM(square, bf16),
         ]
-        + [pltpu.VMEM((square[0], HD), bf16)] * 4
-        + [pltpu.SemaphoreType.DMA((6,))],
+        + [pltpu.VMEM((square[0], HD), bf16)] * 4,
         begin,
         block,
-        place_out=ANY,
     )
     back = exchange(done.reshape(SPREAD, 8, 2048), SEQ_AXES)
     (unsorted,) = call(
@@ -373,10 +355,13 @@
 
 
 def solution(mesh):
-    rows = P(("inner", "outer", "head"), None)
+    parts = {"head": (("z_hi", 4), ("core", 2)), "inner": (("y", 4),), "outer": (("z_lo", 2), ("x", 4))}
+    axes = [part for name in mesh.axis_names for part in parts[name]]
+    split = Mesh(mesh.devices.reshape([size for _, size in axes]), [name for name, _ in axes])
+    rows = P(ROWS, None)
     return jax.shard_map(
         per_device,
-        mesh=mesh,
+        mesh=split,
         in_specs=(rows, rows, rows, rows, P(), P()),
         out_specs=(rows, rows, rows, rows),
         check_vma=False,

time: 122 us -> 119 us (0.975)
  Pallas kernels: 12 us -> 10.6 us
    pallas_call x5, Pallas kernels: 10.7 us -> 9.07 us  [call(): pl.pallas_call(kernel, out_shape=[jax.ShapeDtypeStruct(o, bf16) for o in...]
where the time goes in v2:
time: 119 us
  blocking collectives  70.9 us (60%)
  waiting for transfers between devices  19 us (16%)
  starting transfers between devices  15.7 us (13%)
  Pallas kernels  10.6 us (9%)
  local copies, waits for them, and re-layouts  1.65 us (1%)
    all_to_all x3, blocking collectives, exchange(): return lax.all_to_all(x, axes, split_axis=0, concat_axis=0, tiled=True)  70.9 us
    all_to_all x1, waiting for transfers between devices, exchange(): return lax.all_to_all(x, axes, split_axis=0, concat_axis=0, tiled=True)  19 us
    all_to_all x1, starting transfers between devices, exchange(): return lax.all_to_all(x, axes, split_axis=0, concat_axis=0, tiled=True)  15.7 us
    pallas_call x5, Pallas kernels, call(): pl.pallas_call(kernel, out_shape=[jax.ShapeDtypeStruct(o, bf16) for o in...  9.07 us
  transfers between devices with their start and end apart: 1, of which 1 were waited for; matrix products, arithmetic and copies ran while one was open for 1% of the time, Pallas kernels for 1%

profile of v2, /device:TPU:1, one launch (start us, length us, event | category | flops | bytes accessed | tf_op | source)
XLA Modules:
  0.0 118.6 jit_solution(13240362957974976424)
XLA Ops:
  0.6 2.4 %shard_map.94 = bf16[2560,128]{1,0:T(8,128)(2,1)} custom-call(bf16[30,4096]{1,0:T(8,128)(2,1)} %q_ref.1, bf16[30,1024]{1,0:T(8,128)(2,1)} %k_ref.1, bf16[30,1024]{1,0:T(8,128)(2,1)} %v_ref.1, bf16[30,4096]{1,0:T(8,128)(2,1)} %g_ref.1), custom_call_target="tpu_custom_call" | custom-call | tf_op jit(solution)/shard_map/pallas_call | solution.py:255
  3.0 15.7 %all-to-all-start = ((bf16[256,5,2,128]{3,2,1,0:T(2,128)(2,1)}), bf16[256,5,2,128]{3,2,1,0:T(2,128)(2,1)S(1)}, u32[]{:S(2)}, u32[]{:S(2)}) async-start(bf16[256,5,2,128]{3,2,1,0:T(2,128)(2,1)} %bitcast.17), calls=%async_computation | async-start | bytes 1310720 | tf_op jit(solution)/shard_map/all_to_all | solution.py:266
  18.7 0.9 slice.3
  19.6 0.1 copy.10.run_col_ref
  19.7 0.0 copy-start
  19.7 0.7 copy-done
  20.4 1.6 %shard_map.93 = (bf16[1024,256]{1,0:T(8,128)(2,1)S(1)}, bf16[256,256]{1,0:T(8,128)(2,1)S(1)}, bf16[320,320]{1,0:T(8,128)(2,1)S(1)}, s32[1,256]{1,0:T(1,128)S(1)}) custom-call(s32[1,64]{1,0:T(1,128)S(1)} %get-tuple-element.13.run_row_ref, s32[64,1]{1,0:T(8,128)S(1)} %copy.10.run_col_ref, s32[16]{0:T(128)S(1)} %copy-done), custom_call_target="tpu_custom_call" | custom-call | flops 16777216 | bytes 262144 | tf_op jit(solution)/shard_map/pallas_call | solution.py:287
  21.9 19.0 %all-to-all-done = bf16[256,5,2,128]{3,2,1,0:T(2,128)(2,1)S(1)} async-done(((bf16[256,5,2,128]{3,2,1,0:T(2,128)(2,1)}), bf16[256,5,2,128]{3,2,1,0:T(2,128)(2,1)S(1)}, u32[]{:S(2)}, u32[]{:S(2)}) %all-to-all-start) | async-done | bytes 655392 | tf_op jit(solution)/shard_map/all_to_all | solution.py:266
  41.0 0.6 shard_map.95
  41.6 22.3 %all_to_all.20 = bf16[32,8,2048]{2,1,0:T(8,128)(2,1)S(1)} all-to-all(bf16[32,8,2048]{2,1,0:T(8,128)(2,1)S(1)} %bitcast.11), channel_id=1, replica_groups=mesh['z_hi'=4,'core'=2,'y'=4,'z_lo'=2,'x'=4] {'y','x','core'}, dimensions={0} | all-to-all | bytes 2097152 | tf_op jit(solution)/shard_map/all_to_all | solution.py:266
  63.9 4.3 %shard_map.96 = bf16[256,2048]{1,0:T(8,128)(2,1)S(1)} custom-call(s32[1,256]{1,0:T(1,128)S(1)} %get-tuple-element.8.begin_ref, bf16[256,2048]{1,0:T(8,128)(2,1)S(1)} %bitcast.12), custom_call_target="tpu_custom_call" | custom-call | tf_op jit(solution)/shard_map/pallas_call | solution.py:255
  68.3 20.7 %all_to_all.21.r_ref = bf16[32,8,2048]{2,1,0:T(8,128)(2,1)S(1)} all-to-all(bf16[32,8,2048]{2,1,0:T(8,128)(2,1)S(1)} %bitcast.13), channel_id=1, replica_groups=mesh['z_hi'=4,'core'=2,'y'=4,'z_lo'=2,'x'=4] {'y','x','core'}, dimensions={0} | all-to-all | bytes 2097152 | tf_op jit(solution)/shard_map/all_to_all | solution.py:266
  89.0 0.4 shard_map.97
  89.4 27.9 %all_to_all.22 = bf16[256,5,2,128]{3,2,1,0:T(2,128)(2,1)S(1)} all-to-all(bf16[256,5,2,128]{3,2,1,0:T(2,128)(2,1)S(1)} %bitcast.14), channel_id=1, replica_groups=mesh['z_hi'=4,'core'=2,'y'=4,'z_lo'=2,'x'=4] {'z_hi','z_lo','y','x','core'}, dimensions={0} | all-to-all | bytes 1310720 | tf_op jit(solution)/shard_map/all_to_all | solution.py:266
  117.2 1.3 %shard_map.98 = (bf16[30,4096]{1,0:T(8,128)(2,1)}, bf16[30,4096]{1,0:T(8,128)(2,1)}, bf16[30,1024]{1,0:T(8,128)(2,1)}, bf16[30,1024]{1,0:T(8,128)(2,1)}) custom-call(bf16[2560,128]{1,0:T(8,128)(2,1)S(1)} %bitcast.15, bf16[320,320]{1,0:T(8,128)(2,1)S(1)} %get-tuple-element.11.place_ref), custom_call_target="tpu_custom_call" | custom-call | tf_op jit(solution)/shard_map/pallas_call | solution.py:255
  (2 shorter events, 0.0 us)
Async XLA Ops:
  3.0 37.9 %all-to-all-start = ((bf16[256,5,2,128]{3,2,1,0:T(2,128)(2,1)}), bf16[256,5,2,128]{3,2,1,0:T(2,128)(2,1)S(1)}, u32[]{:S(2)}, u32[]{:S(2)}) async-start(bf16[256,5,2,128]{3,2,1,0:T(2,128)(2,1)} %bitcast.17), calls=%async_computation | async-start | bytes 1310720 | tf_op jit(solution)/shard_map/all_to_all | solution.py:266
  19.7 0.7 copy-start

commit v3 on v2

--- a/solution.py
+++ b/solution.py
@@ -167,7 +167,7 @@
 
 
 def sort_kernel(r_ref, place_ref, out_ref, wide_ref, x_ref):
-    wide_ref[...] = r_ref[...].astype(f32)
+    wide_ref[pl.ds(0, UNIT * BLOCK), :] = r_ref[...].astype(f32)
     for u in range(UNIT):
         x_ref[:, pl.ds(u * HD, HD)] = wide_ref[pl.ds(u, BLOCK, stride=UNIT), :].astype(bf16)
     out_ref[:, pl.ds(0, 1280)] = dot(place_ref[pl.ds(0, BLOCK), :], x_ref[...]).astype(bf16)
@@ -192,7 +192,7 @@
         rows = dot(place_ref[...], x_ref[:, pl.ds(pair * 2 * HD, 2 * HD)])
         wide_ref[pl.ds(2 * pair, BLOCK, stride=UNIT), :] = rows[:, :HD]
         wide_ref[pl.ds(2 * pair + 1, BLOCK, stride=UNIT), :] = rows[:, HD:]
-    out_ref[...] = wide_ref[...].astype(bf16)
+    out_ref[...] = wide_ref[pl.ds(0, UNIT * BLOCK), :].astype(bf16)
 
 
 def attention_kernel(
@@ -220,21 +220,22 @@
     keys, values = k_ref[...], v_ref[...]
     keys_t, values_t = keys.T, values.T
 
-    tops, inverses, deltas = [], [], []
+    tops, accums, inverses, deltas = [], [], [], []
     for g in heads:
         s = dot_nt(keys, q_ref[rows(g), :]) * (SCALE * LOG2E) + bias_ref[...]
         s_ref[:, rows(g)] = s
         tops.append(jnp.max(s, axis=0, keepdims=True))
-        dp_ref[:, rows(g)] = dot_nt(values, g_ref[rows(g), :])
     for g in heads:
         weights = jnp.exp2(s_ref[:, rows(g)] - tops[g])
         s_ref[:, rows(g)] = weights
-        inverse = 1.0 / jnp.sum(weights, axis=0, keepdims=True)
-        output = (dot(values_t, weights.astype(bf16)) * inverse).T.astype(bf16)
+        inverses.append(1.0 / jnp.sum(weights, axis=0, keepdims=True))
+        accums.append(dot(values_t, weights.astype(bf16)))
+        dp_ref[:, rows(g)] = dot_nt(values, g_ref[rows(g), :])
+    for g in heads:
+        output = (accums[g] * inverses[g]).T.astype(bf16)
         out_ref[:, pl.ds(g * HD, HD)] = output
         product = g_ref[rows(g), :].astype(f32) * output.astype(f32)
         deltas.append(jnp.sum(product.T, axis=0, keepdims=True))
-        inverses.append(inverse)
     for g in heads:
         prob = s_ref[:, rows(g)] * inverses[g]
         p_ref[:, rows(g)] = prob.astype(bf16)
@@ -309,7 +310,7 @@
     (ordered,) = call(
         sort_kernel,
         [(BLOCK, 2048)],
-        [pltpu.VMEM((units, HD), f32), pltpu.VMEM((BLOCK, 1280), bf16)],
+        [pltpu.VMEM((units + 16, HD), f32), pltpu.VMEM((BLOCK, 1280), bf16)],
         spread,
         place_sort,
     )
@@ -334,7 +335,7 @@
         unsort_kernel,
         [(units, HD)],
         [
-            pltpu.VMEM((units, HD), f32),
+            pltpu.VMEM((units + 16, HD), f32),
             pltpu.VMEM((BLOCK, 256), f32),
             pltpu.VMEM((BLOCK, 1280), bf16),
         ],

time: 119 us -> 119 us (level)
  no operation moved by 1% of the time
where the time goes in v3:
time: 119 us; the launch traced here: 118 us
  blocking collectives  70.9 us (60%)
  waiting for transfers between devices  19 us (16%)
  starting transfers between devices  15.7 us (13%)
  Pallas kernels  10.4 us (9%)
  local copies, waits for them, and re-layouts  1.65 us (1%)
    all_to_all x3, blocking collectives, exchange(): return lax.all_to_all(x, axes, split_axis=0, concat_axis=0, tiled=True)  70.9 us
    all_to_all x1, waiting for transfers between devices, exchange(): return lax.all_to_all(x, axes, split_axis=0, concat_axis=0, tiled=True)  19 us
    all_to_all x1, starting transfers between devices, exchange(): return lax.all_to_all(x, axes, split_axis=0, concat_axis=0, tiled=True)  15.7 us
    pallas_call x5, Pallas kernels, call(): pl.pallas_call(kernel, out_shape=[jax.ShapeDtypeStruct(o, bf16) for o in...  8.87 us
  transfers between devices with their start and end apart: 1, of which 1 were waited for; matrix products, arithmetic and copies ran while one was open for 1% of the time, Pallas kernels for 1%

profile of v3, /device:TPU:1, one launch (start us, length us, event | category | flops | bytes accessed | tf_op | source)
XLA Modules:
  0.0 118.4 jit_solution(3110345136520176837)
XLA Ops:
  0.6 2.4 %shard_map.94 = bf16[2560,128]{1,0:T(8,128)(2,1)} custom-call(bf16[30,4096]{1,0:T(8,128)(2,1)} %q_ref.1, bf16[30,1024]{1,0:T(8,128)(2,1)} %k_ref.1, bf16[30,1024]{1,0:T(8,128)(2,1)} %v_ref.1, bf16[30,4096]{1,0:T(8,128)(2,1)} %g_ref.1), custom_call_target="tpu_custom_call" | custom-call | tf_op jit(solution)/shard_map/pallas_call | solution.py:256
  3.0 15.7 %all-to-all-start = ((bf16[256,5,2,128]{3,2,1,0:T(2,128)(2,1)}), bf16[256,5,2,128]{3,2,1,0:T(2,128)(2,1)S(1)}, u32[]{:S(2)}, u32[]{:S(2)}) async-start(bf16[256,5,2,128]{3,2,1,0:T(2,128)(2,1)} %bitcast.17), calls=%async_computation | async-start | bytes 1310720 | tf_op jit(solution)/shard_map/all_to_all | solution.py:267
  18.7 0.9 slice.3
  19.6 0.1 copy.10.run_col_ref
  19.7 0.0 copy-start
  19.7 0.7 copy-done
  20.4 1.6 %shard_map.93 = (bf16[1024,256]{1,0:T(8,128)(2,1)S(1)}, bf16[256,256]{1,0:T(8,128)(2,1)S(1)}, bf16[320,320]{1,0:T(8,128)(2,1)S(1)}, s32[1,256]{1,0:T(1,128)S(1)}) custom-call(s32[1,64]{1,0:T(1,128)S(1)} %get-tuple-element.13.run_row_ref, s32[64,1]{1,0:T(8,128)S(1)} %copy.10.run_col_ref, s32[16]{0:T(128)S(1)} %copy-done), custom_call_target="tpu_custom_call" | custom-call | flops 16777216 | bytes 262144 | tf_op jit(solution)/shard_map/pallas_call | solution.py:288
  21.9 19.0 %all-to-all-done = bf16[256,5,2,128]{3,2,1,0:T(2,128)(2,1)S(1)} async-done(((bf16[256,5,2,128]{3,2,1,0:T(2,128)(2,1)}), bf16[256,5,2,128]{3,2,1,0:T(2,128)(2,1)S(1)}, u32[]{:S(2)}, u32[]{:S(2)}) %all-to-all-start) | async-done | bytes 655392 | tf_op jit(solution)/shard_map/all_to_all | solution.py:267
  41.0 0.6 shard_map.95
  41.6 22.3 %all_to_all.20 = bf16[32,8,2048]{2,1,0:T(8,128)(2,1)S(1)} all-to-all(bf16[32,8,2048]{2,1,0:T(8,128)(2,1)S(1)} %bitcast.11), channel_id=1, replica_groups=mesh['z_hi'=4,'core'=2,'y'=4,'z_lo'=2,'x'=4] {'y','x','core'}, dimensions={0} | all-to-all | bytes 2097152 | tf_op jit(solution)/shard_map/all_to_all | solution.py:267
  63.9 4.1 %shard_map.96 = bf16[256,2048]{1,0:T(8,128)(2,1)S(1)} custom-call(s32[1,256]{1,0:T(1,128)S(1)} %get-tuple-element.8.begin_ref, bf16[256,2048]{1,0:T(8,128)(2,1)S(1)} %bitcast.12), custom_call_target="tpu_custom_call" | custom-call | tf_op jit(solution)/shard_map/pallas_call | solution.py:256
  68.1 20.7 %all_to_all.21.r_ref = bf16[32,8,2048]{2,1,0:T(8,128)(2,1)S(1)} all-to-all(bf16[32,8,2048]{2,1,0:T(8,128)(2,1)S(1)} %bitcast.13), channel_id=1, replica_groups=mesh['z_hi'=4,'core'=2,'y'=4,'z_lo'=2,'x'=4] {'y','x','core'}, dimensions={0} | all-to-all | bytes 2097152 | tf_op jit(solution)/shard_map/all_to_all | solution.py:267
  88.8 0.4 shard_map.97
  89.2 27.9 %all_to_all.22 = bf16[256,5,2,128]{3,2,1,0:T(2,128)(2,1)S(1)} all-to-all(bf16[256,5,2,128]{3,2,1,0:T(2,128)(2,1)S(1)} %bitcast.14), channel_id=1, replica_groups=mesh['z_hi'=4,'core'=2,'y'=4,'z_lo'=2,'x'=4] {'z_hi','z_lo','y','x','core'}, dimensions={0} | all-to-all | bytes 1310720 | tf_op jit(solution)/shard_map/all_to_all | solution.py:267
  117.0 1.3 %shard_map.98 = (bf16[30,4096]{1,0:T(8,128)(2,1)}, bf16[30,4096]{1,0:T(8,128)(2,1)}, bf16[30,1024]{1,0:T(8,128)(2,1)}, bf16[30,1024]{1,0:T(8,128)(2,1)}) custom-call(bf16[2560,128]{1,0:T(8,128)(2,1)S(1)} %bitcast.15, bf16[320,320]{1,0:T(8,128)(2,1)S(1)} %get-tuple-element.11.place_ref), custom_call_target="tpu_custom_call" | custom-call | tf_op jit(solution)/shard_map/pallas_call | solution.py:256
  (2 shorter events, 0.0 us)
Async XLA Ops:
  3.0 37.9 %all-to-all-start = ((bf16[256,5,2,128]{3,2,1,0:T(2,128)(2,1)}), bf16[256,5,2,128]{3,2,1,0:T(2,128)(2,1)S(1)}, u32[]{:S(2)}, u32[]{:S(2)}) async-start(bf16[256,5,2,128]{3,2,1,0:T(2,128)(2,1)} %bitcast.17), calls=%async_computation | async-start | bytes 1310720 | tf_op jit(solution)/shard_map/all_to_all | solution.py:267
  19.7 0.7 copy-start

commit v4 on v3

--- a/solution.py
+++ b/solution.py
@@ -197,6 +197,7 @@
 
 def attention_kernel(
     begin_ref, m_ref, out_ref, bias_ref, s_ref, dp_ref, p_ref, d_ref, q_ref, g_ref, k_ref, v_ref,
+    dk_ref, dv_ref,
 ):
     base = seq_index() * BLOCK
     blocks, heads = range(BACK + 1), range(GROUP)
@@ -220,32 +221,53 @@
     keys, values = k_ref[...], v_ref[...]
     keys_t, values_t = keys.T, values.T
 
-    tops, accums, inverses, deltas = [], [], [], []
-    for g in heads:
+    tops, accums, inverses, deltas = {}, {}, {}, {}
+
+    def score(g):
         s = dot_nt(keys, q_ref[rows(g), :]) * (SCALE * LOG2E) + bias_ref[...]
         s_ref[:, rows(g)] = s
-        tops.append(jnp.max(s, axis=0, keepdims=True))
-    for g in heads:
+        tops[g] = jnp.max(s, axis=0, keepdims=True)
+
+    def weigh(g):
         weights = jnp.exp2(s_ref[:, rows(g)] - tops[g])
         s_ref[:, rows(g)] = weights
-        inverses.append(1.0 / jnp.sum(weights, axis=0, keepdims=True))
-        accums.append(dot(values_t, weights.astype(bf16)))
+        inverses[g] = 1.0 / jnp.sum(weights, axis=0, keepdims=True)
+        accums[g] = dot(values_t, weights.astype(bf16))
         dp_ref[:, rows(g)] = dot_nt(values, g_ref[rows(g), :])
-    for g in heads:
+
+    def attend(g):
         output = (accums[g] * inverses[g]).T.astype(bf16)
         out_ref[:, pl.ds(g * HD, HD)] = output
         product = g_ref[rows(g), :].astype(f32) * output.astype(f32)
-        deltas.append(jnp.sum(product.T, axis=0, keepdims=True))
-    for g in heads:
+        deltas[g] = jnp.sum(product.T, axis=0, keepdims=True)
+
+    def back(g):
         prob = s_ref[:, rows(g)] * inverses[g]
         p_ref[:, rows(g)] = prob.astype(bf16)
         dscore = (prob * (dp_ref[:, rows(g)] - deltas[g])).astype(bf16)
         d_ref[:, rows(g)] = dscore
         out_ref[:, pl.ds((GROUP + g) * HD, HD)] = (dot(keys_t, dscore) * SCALE).T.astype(bf16)
-    for b in blocks:
-        at = 2 * GROUP * HD + 2 * HD * b
-        out_ref[:, pl.ds(at, HD)] = (dot(d_ref[rows(b), :], q_ref[...]) * SCALE).astype(bf16)
-        out_ref[:, pl.ds(at + HD, HD)] = dot(p_ref[rows(b), :], g_ref[...]).astype(bf16)
+
+    def key_grads(half):
+        two = pl.ds(half * 2 * BLOCK, 2 * BLOCK)
+        for b in blocks:
+            key_term = dot(d_ref[rows(b), two], q_ref[two, :])
+            value_term = dot(p_ref[rows(b), two], g_ref[two, :])
+            if half == 0:
+                dk_ref[rows(b), :] = key_term
+                dv_ref[rows(b), :] = value_term
+            else:
+                at = 2 * GROUP * HD + 2 * HD * b
+                key_term = (dk_ref[rows(b), :] + key_term) * SCALE
+                out_ref[:, pl.ds(at, HD)] = key_term.astype(bf16)
+                out_ref[:, pl.ds(at + HD, HD)] = (dv_ref[rows(b), :] + value_term).astype(bf16)
+
+    for step, g in (
+        (score, 0), (score, 1), (weigh, 0), (score, 2), (weigh, 1), (attend, 0), (score, 3),
+        (weigh, 2), (attend, 1), (back, 0), (weigh, 3), (attend, 2), (back, 1), (key_grads, 0),
+        (attend, 3), (back, 2), (back, 3), (key_grads, 1),
+    ):
+        step(g)
 
 
 VMEM = pl.BlockSpec(memory_space=pltpu.VMEM)
@@ -326,7 +348,8 @@
             pltpu.VMEM(square, bf16),
             pltpu.VMEM(square, bf16),
         ]
-        + [pltpu.VMEM((square[0], HD), bf16)] * 4,
+        + [pltpu.VMEM((square[0], HD), bf16)] * 4
+        + [pltpu.VMEM((square[1], HD), f32)] * 2,
         begin,
         block,
     )

time: 119 us -> 119 us (level)
  no operation moved by 1% of the time
where the time goes in v4:
time: 119 us; the launch traced here: 118 us
  blocking collectives  70.9 us (60%)
  waiting for transfers between devices  19 us (16%)
  starting transfers between devices  15.7 us (13%)
  Pallas kernels  10.3 us (9%)
  local copies, waits for them, and re-layouts  1.65 us (1%)
    all_to_all x3, blocking collectives, exchange(): return lax.all_to_all(x, axes, split_axis=0, concat_axis=0, tiled=True)  70.9 us
    all_to_all x1, waiting for transfers between devices, exchange(): return lax.all_to_all(x, axes, split_axis=0, concat_axis=0, tiled=True)  19 us
    all_to_all x1, starting transfers between devices, exchange(): return lax.all_to_all(x, axes, split_axis=0, concat_axis=0, tiled=True)  15.7 us
    pallas_call x5, Pallas kernels, call(): pl.pallas_call(kernel, out_shape=[jax.ShapeDtypeStruct(o, bf16) for o in...  8.7 us
  transfers between devices with their start and end apart: 1, of which 1 were waited for; matrix products, arithmetic and copies ran while one was open for 1% of the time, Pallas kernels for 1%

profile of v4, /device:TPU:1, one launch (start us, length us, event | category | flops | bytes accessed | tf_op | source)
XLA Modules:
  0.0 118.2 jit_solution(7256114155085572484)
XLA Ops:
  0.6 2.4 %shard_map.94 = bf16[2560,128]{1,0:T(8,128)(2,1)} custom-call(bf16[30,4096]{1,0:T(8,128)(2,1)} %q_ref.1, bf16[30,1024]{1,0:T(8,128)(2,1)} %k_ref.1, bf16[30,1024]{1,0:T(8,128)(2,1)} %v_ref.1, bf16[30,4096]{1,0:T(8,128)(2,1)} %g_ref.1), custom_call_target="tpu_custom_call" | custom-call | tf_op jit(solution)/shard_map/pallas_call | solution.py:278
  3.0 15.7 %all-to-all-start = ((bf16[256,5,2,128]{3,2,1,0:T(2,128)(2,1)}), bf16[256,5,2,128]{3,2,1,0:T(2,128)(2,1)S(1)}, u32[]{:S(2)}, u32[]{:S(2)}) async-start(bf16[256,5,2,128]{3,2,1,0:T(2,128)(2,1)} %bitcast.17), calls=%async_computation | async-start | bytes 1310720 | tf_op jit(solution)/shard_map/all_to_all | solution.py:289
  18.7 0.9 slice.3
  19.6 0.1 copy.10.run_col_ref
  19.7 0.0 copy-start
  19.7 0.7 copy-done
  20.4 1.6 %shard_map.93 = (bf16[1024,256]{1,0:T(8,128)(2,1)S(1)}, bf16[256,256]{1,0:T(8,128)(2,1)S(1)}, bf16[320,320]{1,0:T(8,128)(2,1)S(1)}, s32[1,256]{1,0:T(1,128)S(1)}) custom-call(s32[1,64]{1,0:T(1,128)S(1)} %get-tuple-element.13.run_row_ref, s32[64,1]{1,0:T(8,128)S(1)} %copy.10.run_col_ref, s32[16]{0:T(128)S(1)} %copy-done), custom_call_target="tpu_custom_call" | custom-call | flops 16777216 | bytes 262144 | tf_op jit(solution)/shard_map/pallas_call | solution.py:310
  21.9 19.0 %all-to-all-done = bf16[256,5,2,128]{3,2,1,0:T(2,128)(2,1)S(1)} async-done(((bf16[256,5,2,128]{3,2,1,0:T(2,128)(2,1)}), bf16[256,5,2,128]{3,2,1,0:T(2,128)(2,1)S(1)}, u32[]{:S(2)}, u32[]{:S(2)}) %all-to-all-start) | async-done | bytes 655392 | tf_op jit(solution)/shard_map/all_to_all | solution.py:289
  41.0 0.6 shard_map.95
  41.6 22.3 %all_to_all.20 = bf16[32,8,2048]{2,1,0:T(8,128)(2,1)S(1)} all-to-all(bf16[32,8,2048]{2,1,0:T(8,128)(2,1)S(1)} %bitcast.11), channel_id=1, replica_groups=mesh['z_hi'=4,'core'=2,'y'=4,'z_lo'=2,'x'=4] {'y','x','core'}, dimensions={0} | all-to-all | bytes 2097152 | tf_op jit(solution)/shard_map/all_to_all | solution.py:289
  63.9 4.0 %shard_map.96 = bf16[256,2048]{1,0:T(8,128)(2,1)S(1)} custom-call(s32[1,256]{1,0:T(1,128)S(1)} %get-tuple-element.8.begin_ref, bf16[256,2048]{1,0:T(8,128)(2,1)S(1)} %bitcast.12), custom_call_target="tpu_custom_call" | custom-call | tf_op jit(solution)/shard_map/pallas_call | solution.py:278
  67.9 20.7 %all_to_all.21.r_ref = bf16[32,8,2048]{2,1,0:T(8,128)(2,1)S(1)} all-to-all(bf16[32,8,2048]{2,1,0:T(8,128)(2,1)S(1)} %bitcast.13), channel_id=1, replica_groups=mesh['z_hi'=4,'core'=2,'y'=4,'z_lo'=2,'x'=4] {'y','x','core'}, dimensions={0} | all-to-all | bytes 2097152 | tf_op jit(solution)/shard_map/all_to_all | solution.py:289
  88.6 0.4 shard_map.97
  89.0 27.9 %all_to_all.22 = bf16[256,5,2,128]{3,2,1,0:T(2,128)(2,1)S(1)} all-to-all(bf16[256,5,2,128]{3,2,1,0:T(2,128)(2,1)S(1)} %bitcast.14), channel_id=1, replica_groups=mesh['z_hi'=4,'core'=2,'y'=4,'z_lo'=2,'x'=4] {'z_hi','z_lo','y','x','core'}, dimensions={0} | all-to-all | bytes 1310720 | tf_op jit(solution)/shard_map/all_to_all | solution.py:289
  116.9 1.3 %shard_map.98 = (bf16[30,4096]{1,0:T(8,128)(2,1)}, bf16[30,4096]{1,0:T(8,128)(2,1)}, bf16[30,1024]{1,0:T(8,128)(2,1)}, bf16[30,1024]{1,0:T(8,128)(2,1)}) custom-call(bf16[2560,128]{1,0:T(8,128)(2,1)S(1)} %bitcast.15, bf16[320,320]{1,0:T(8,128)(2,1)S(1)} %get-tuple-element.11.place_ref), custom_call_target="tpu_custom_call" | custom-call | tf_op jit(solution)/shard_map/pallas_call | solution.py:278
  (2 shorter events, 0.0 us)
Async XLA Ops:
  3.0 37.9 %all-to-all-start = ((bf16[256,5,2,128]{3,2,1,0:T(2,128)(2,1)}), bf16[256,5,2,128]{3,2,1,0:T(2,128)(2,1)S(1)}, u32[]{:S(2)}, u32[]{:S(2)}) async-start(bf16[256,5,2,128]{3,2,1,0:T(2,128)(2,1)} %bitcast.17), calls=%async_computation | async-start | bytes 1310720 | tf_op jit(solution)/shard_map/all_to_all | solution.py:289
  19.7 0.7 copy-start

commit v5 on v4

--- a/solution.py
+++ b/solution.py
@@ -99,15 +99,20 @@
 
 def unpack_kernel(r_ref, place_ref, att_ref, gq_ref, gk_ref, gv_ref, qs, ks, vs, gs, x_ref, sem):
     size = UNIT * 32
-    wide, pairs = 2 * GROUP * HD, KVH // 2
+    pairs, half = KVH // 2, KVH * GROUP * HD // 2
     departures = []
+
+    def send(source, to):
+        departures.append(pltpu.make_async_copy(source, to, sem.at[len(departures)]))
+        departures[-1].start()
+
     for pair in range(pairs):
-        for half in range(2):
-            x_ref[pair, :, pl.ds(half * HD, HD)] = r_ref[pl.ds((2 * pair + half) * size, size), :]
-        rows = dot(place_ref[...], x_ref[pair]).astype(bf16)
-        for half in range(2):
-            head = 2 * pair + half
-            part = rows[:, half * HD : (half + 1) * HD]
+        two = pl.ds(pair * 2 * HD, 2 * HD)
+        for head in (2 * pair, 2 * pair + 1):
+            x_ref[:, pl.ds(head * HD, HD)] = r_ref[pl.ds(head * size, size), :]
+        rows = dot(place_ref[...], x_ref[:, two]).astype(bf16)
+        for head in (2 * pair, 2 * pair + 1):
+            part = rows[:, :HD] if head % 2 == 0 else rows[:, HD:]
             to = pl.ds(head * HD, HD)
             for g in range(GROUP):
                 column = pl.ds((head * GROUP + g) * HD, HD)
@@ -115,15 +120,12 @@
                 gs[:, column] = part[(GROUP + g) * 32 : (GROUP + g) * 32 + LOCAL]
             ks[:, to] = part[8 * 32 : 8 * 32 + LOCAL]
             vs[:, to] = part[9 * 32 : 9 * 32 + LOCAL]
-        at = pl.ds(pair * wide, wide)
-        for source, to in ((qs, att_ref), (gs, gq_ref)):
-            departures.append(
-                pltpu.make_async_copy(source.at[:, at], to.at[:, at], sem.at[len(departures)])
-            )
-            departures[-1].start()
-    for source, to in ((ks, gk_ref), (vs, gv_ref)):
-        departures.append(pltpu.make_async_copy(source, to, sem.at[len(departures)]))
-        departures[-1].start()
+        if pair % 2 == 1:
+            at = pl.ds(pair // 2 * half, half)
+            send(qs.at[:, at], att_ref.at[:, at])
+            send(gs.at[:, at], gq_ref.at[:, at])
+    send(ks, gk_ref)
+    send(vs, gv_ref)
     for copy in departures:
         copy.wait()
 
@@ -370,7 +372,7 @@
         call(
             unpack_kernel,
             [wide, wide, narrow, narrow],
-            local + [pltpu.VMEM((4, size, 2 * HD), bf16), pltpu.SemaphoreType.DMA((10,))],
+            local + [pltpu.VMEM((size, KVH * HD), bf16), pltpu.SemaphoreType.DMA((6,))],
             home,
             place_unpack,
             place_out=ANY,

time: 119 us -> 118 us (level)
  no operation moved by 1% of the time
where the time goes in v5:
time: 118 us
  blocking collectives  70.9 us (60%)
  waiting for transfers between devices  19 us (16%)
  starting transfers between devices  15.7 us (13%)
  Pallas kernels  10.2 us (9%)
  local copies, waits for them, and re-layouts  1.65 us (1%)
    all_to_all x3, blocking collectives, exchange(): return lax.all_to_all(x, axes, split_axis=0, concat_axis=0, tiled=True)  70.9 us
    all_to_all x1, waiting for transfers between devices, exchange(): return lax.all_to_all(x, axes, split_axis=0, concat_axis=0, tiled=True)  19 us
    all_to_all x1, starting transfers between devices, exchange(): return lax.all_to_all(x, axes, split_axis=0, concat_axis=0, tiled=True)  15.7 us
    pallas_call x5, Pallas kernels, call(): pl.pallas_call(kernel, out_shape=[jax.ShapeDtypeStruct(o, bf16) for o in...  8.66 us
  transfers between devices with their start and end apart: 1, of which 1 were waited for; matrix products, arithmetic and copies ran while one was open for 1% of the time, Pallas kernels for 1%

profile of v5, /device:TPU:1, one launch (start us, length us, event | category | flops | bytes accessed | tf_op | source)
XLA Modules:
  0.0 118.2 jit_solution(18357097444816451382)
XLA Ops:
  0.6 2.4 %shard_map.94 = bf16[2560,128]{1,0:T(8,128)(2,1)} custom-call(bf16[30,4096]{1,0:T(8,128)(2,1)} %q_ref.1, bf16[30,1024]{1,0:T(8,128)(2,1)} %k_ref.1, bf16[30,1024]{1,0:T(8,128)(2,1)} %v_ref.1, bf16[30,4096]{1,0:T(8,128)(2,1)} %g_ref.1), custom_call_target="tpu_custom_call" | custom-call | tf_op jit(solution)/shard_map/pallas_call | solution.py:280
  3.0 15.7 %all-to-all-start = ((bf16[256,5,2,128]{3,2,1,0:T(2,128)(2,1)}), bf16[256,5,2,128]{3,2,1,0:T(2,128)(2,1)S(1)}, u32[]{:S(2)}, u32[]{:S(2)}) async-start(bf16[256,5,2,128]{3,2,1,0:T(2,128)(2,1)} %bitcast.17), calls=%async_computation | async-start | bytes 1310720 | tf_op jit(solution)/shard_map/all_to_all | solution.py:291
  18.7 0.9 slice.3
  19.6 0.1 copy.10.run_col_ref
  19.7 0.0 copy-start
  19.7 0.7 copy-done
  20.4 1.6 %shard_map.93 = (bf16[1024,256]{1,0:T(8,128)(2,1)S(1)}, bf16[256,256]{1,0:T(8,128)(2,1)S(1)}, bf16[320,320]{1,0:T(8,128)(2,1)S(1)}, s32[1,256]{1,0:T(1,128)S(1)}) custom-call(s32[1,64]{1,0:T(1,128)S(1)} %get-tuple-element.13.run_row_ref, s32[64,1]{1,0:T(8,128)S(1)} %copy.10.run_col_ref, s32[16]{0:T(128)S(1)} %copy-done), custom_call_target="tpu_custom_call" | custom-call | flops 16777216 | bytes 262144 | tf_op jit(solution)/shard_map/pallas_call | solution.py:312
  21.9 19.0 %all-to-all-done = bf16[256,5,2,128]{3,2,1,0:T(2,128)(2,1)S(1)} async-done(((bf16[256,5,2,128]{3,2,1,0:T(2,128)(2,1)}), bf16[256,5,2,128]{3,2,1,0:T(2,128)(2,1)S(1)}, u32[]{:S(2)}, u32[]{:S(2)}) %all-to-all-start) | async-done | bytes 655392 | tf_op jit(solution)/shard_map/all_to_all | solution.py:291
  41.0 0.6 shard_map.95
  41.6 22.3 %all_to_all.20 = bf16[32,8,2048]{2,1,0:T(8,128)(2,1)S(1)} all-to-all(bf16[32,8,2048]{2,1,0:T(8,128)(2,1)S(1)} %bitcast.11), channel_id=1, replica_groups=mesh['z_hi'=4,'core'=2,'y'=4,'z_lo'=2,'x'=4] {'y','x','core'}, dimensions={0} | all-to-all | bytes 2097152 | tf_op jit(solution)/shard_map/all_to_all | solution.py:291
  63.9 4.0 %shard_map.96 = bf16[256,2048]{1,0:T(8,128)(2,1)S(1)} custom-call(s32[1,256]{1,0:T(1,128)S(1)} %get-tuple-element.8.begin_ref, bf16[256,2048]{1,0:T(8,128)(2,1)S(1)} %bitcast.12), custom_call_target="tpu_custom_call" | custom-call | tf_op jit(solution)/shard_map/pallas_call | solution.py:280
  67.9 20.7 %all_to_all.21.r_ref = bf16[32,8,2048]{2,1,0:T(8,128)(2,1)S(1)} all-to-all(bf16[32,8,2048]{2,1,0:T(8,128)(2,1)S(1)} %bitcast.13), channel_id=1, replica_groups=mesh['z_hi'=4,'core'=2,'y'=4,'z_lo'=2,'x'=4] {'y','x','core'}, dimensions={0} | all-to-all | bytes 2097152 | tf_op jit(solution)/shard_map/all_to_all | solution.py:291
  88.6 0.4 shard_map.97
  89.0 27.9 %all_to_all.22 = bf16[256,5,2,128]{3,2,1,0:T(2,128)(2,1)S(1)} all-to-all(bf16[256,5,2,128]{3,2,1,0:T(2,128)(2,1)S(1)} %bitcast.14), channel_id=1, replica_groups=mesh['z_hi'=4,'core'=2,'y'=4,'z_lo'=2,'x'=4] {'z_hi','z_lo','y','x','core'}, dimensions={0} | all-to-all | bytes 1310720 | tf_op jit(solution)/shard_map/all_to_all | solution.py:291
  116.9 1.3 %shard_map.98 = (bf16[30,4096]{1,0:T(8,128)(2,1)}, bf16[30,4096]{1,0:T(8,128)(2,1)}, bf16[30,1024]{1,0:T(8,128)(2,1)}, bf16[30,1024]{1,0:T(8,128)(2,1)}) custom-call(bf16[2560,128]{1,0:T(8,128)(2,1)S(1)} %bitcast.15, bf16[320,320]{1,0:T(8,128)(2,1)S(1)} %get-tuple-element.11.place_ref), custom_call_target="tpu_custom_call" | custom-call | tf_op jit(solution)/shard_map/pallas_call | solution.py:280
  (2 shorter events, 0.0 us)
Async XLA Ops:
  3.0 37.9 %all-to-all-start = ((bf16[256,5,2,128]{3,2,1,0:T(2,128)(2,1)}), bf16[256,5,2,128]{3,2,1,0:T(2,128)(2,1)S(1)}, u32[]{:S(2)}, u32[]{:S(2)}) async-start(bf16[256,5,2,128]{3,2,1,0:T(2,128)(2,1)} %bitcast.17), calls=%async_computation | async-start | bytes 1310720 | tf_op jit(solution)/shard_map/all_to_all | solution.py:291
  19.7 0.7 copy-start

commit v6 on v5

--- a/solution.py
+++ b/solution.py
@@ -198,8 +198,7 @@
 
 
 def attention_kernel(
-    begin_ref, m_ref, out_ref, bias_ref, s_ref, dp_ref, p_ref, d_ref, q_ref, g_ref, k_ref, v_ref,
-    dk_ref, dv_ref,
+    begin_ref, m_ref, out_ref, bias_ref, s_ref, dp_ref, p_ref, d_ref, dk_ref, dv_ref,
 ):
     base = seq_index() * BLOCK
     blocks, heads = range(BACK + 1), range(GROUP)
@@ -215,18 +214,20 @@
         if b == 0:
             seen = seen & (key_pos <= query_pos)
         bias_ref[rows(b), :] = jnp.where(seen, 0.0, NEGATIVE)
-        k_ref[rows(b), :] = m_ref[:, pl.ds(1024 + 256 * b, HD)]
-        v_ref[rows(b), :] = m_ref[:, pl.ds(1024 + 256 * b + HD, HD)]
-    for g in heads:
-        q_ref[rows(g), :] = m_ref[:, pl.ds(g * HD, HD)]
-        g_ref[rows(g), :] = m_ref[:, pl.ds((GROUP + g) * HD, HD)]
-    keys, values = k_ref[...], v_ref[...]
+
+    def joined(first, count, step=HD):
+        parts = [m_ref[:, pl.ds(first + step * i, HD)] for i in range(count)]
+        return jnp.concatenate(parts, axis=0)
+
+    keys, values = joined(2 * GROUP * HD, BACK + 1, 2 * HD), joined(2 * GROUP * HD + HD, BACK + 1, 2 * HD)
+    queries = [m_ref[:, pl.ds(g * HD, HD)] for g in heads]
+    grads = [m_ref[:, pl.ds((GROUP + g) * HD, HD)] for g in heads]
     keys_t, values_t = keys.T, values.T
 
     tops, accums, inverses, deltas = {}, {}, {}, {}
 
     def score(g):
-        s = dot_nt(keys, q_ref[rows(g), :]) * (SCALE * LOG2E) + bias_ref[...]
+        s = dot_nt(keys, queries[g]) * (SCALE * LOG2E) + bias_ref[...]
         s_ref[:, rows(g)] = s
         tops[g] = jnp.max(s, axis=0, keepdims=True)
 
@@ -235,12 +236,12 @@
         s_ref[:, rows(g)] = weights
         inverses[g] = 1.0 / jnp.sum(weights, axis=0, keepdims=True)
         accums[g] = dot(values_t, weights.astype(bf16))
-        dp_ref[:, rows(g)] = dot_nt(values, g_ref[rows(g), :])
+        dp_ref[:, rows(g)] = dot_nt(values, grads[g])
 
     def attend(g):
         output = (accums[g] * inverses[g]).T.astype(bf16)
         out_ref[:, pl.ds(g * HD, HD)] = output
-        product = g_ref[rows(g), :].astype(f32) * output.astype(f32)
+        product = grads[g].astype(f32) * output.astype(f32)
         deltas[g] = jnp.sum(product.T, axis=0, keepdims=True)
 
     def back(g):
@@ -252,9 +253,10 @@
 
     def key_grads(half):
         two = pl.ds(half * 2 * BLOCK, 2 * BLOCK)
+        query, grad = joined(half * 2 * HD, 2), joined((GROUP + 2 * half) * HD, 2)
         for b in blocks:
-            key_term = dot(d_ref[rows(b), two], q_ref[two, :])
-            value_term = dot(p_ref[rows(b), two], g_ref[two, :])
+            key_term = dot(d_ref[rows(b), two], query)
+            value_term = dot(p_ref[rows(b), two], grad)
             if half == 0:
                 dk_ref[rows(b), :] = key_term
                 dv_ref[rows(b), :] = value_term
@@ -350,7 +352,6 @@
             pltpu.VMEM(square, bf16),
             pltpu.VMEM(square, bf16),
         ]
-        + [pltpu.VMEM((square[0], HD), bf16)] * 4
         + [pltpu.VMEM((square[1], HD), f32)] * 2,
         begin,
         block,

time: 118 us -> 118 us (level)
  no operation moved by 1% of the time
where the time goes in v6:
time: 118 us
  blocking collectives  70.9 us (60%)
  waiting for transfers between devices  19 us (16%)
  starting transfers between devices  15.7 us (13%)
  Pallas kernels  10 us (8%)
  local copies, waits for them, and re-layouts  1.65 us (1%)
    all_to_all x3, blocking collectives, exchange(): return lax.all_to_all(x, axes, split_axis=0, concat_axis=0, tiled=True)  70.9 us
    all_to_all x1, waiting for transfers between devices, exchange(): return lax.all_to_all(x, axes, split_axis=0, concat_axis=0, tiled=True)  19 us
    all_to_all x1, starting transfers between devices, exchange(): return lax.all_to_all(x, axes, split_axis=0, concat_axis=0, tiled=True)  15.7 us
    pallas_call x5, Pallas kernels, call(): pl.pallas_call(kernel, out_shape=[jax.ShapeDtypeStruct(o, bf16) for o in...  8.48 us
  transfers between devices with their start and end apart: 1, of which 1 were waited for; matrix products, arithmetic and copies ran while one was open for 1% of the time, Pallas kernels for 1%

profile of v6, /device:TPU:1, one launch (start us, length us, event | category | flops | bytes accessed | tf_op | source)
XLA Modules:
  0.0 118.0 jit_solution(14046804779056239437)
XLA Ops:
  0.6 2.4 %shard_map.94 = bf16[2560,128]{1,0:T(8,128)(2,1)} custom-call(bf16[30,4096]{1,0:T(8,128)(2,1)} %q_ref.1, bf16[30,1024]{1,0:T(8,128)(2,1)} %k_ref.1, bf16[30,1024]{1,0:T(8,128)(2,1)} %v_ref.1, bf16[30,4096]{1,0:T(8,128)(2,1)} %g_ref.1), custom_call_target="tpu_custom_call" | custom-call | tf_op jit(solution)/shard_map/pallas_call | solution.py:282
  3.0 15.7 %all-to-all-start = ((bf16[256,5,2,128]{3,2,1,0:T(2,128)(2,1)}), bf16[256,5,2,128]{3,2,1,0:T(2,128)(2,1)S(1)}, u32[]{:S(2)}, u32[]{:S(2)}) async-start(bf16[256,5,2,128]{3,2,1,0:T(2,128)(2,1)} %bitcast.17), calls=%async_computation | async-start | bytes 1310720 | tf_op jit(solution)/shard_map/all_to_all | solution.py:293
  18.7 0.9 slice.3
  19.6 0.1 copy.10.run_col_ref
  19.7 0.0 copy-start
  19.7 0.7 copy-done
  20.4 1.6 %shard_map.93 = (bf16[1024,256]{1,0:T(8,128)(2,1)S(1)}, bf16[256,256]{1,0:T(8,128)(2,1)S(1)}, bf16[320,320]{1,0:T(8,128)(2,1)S(1)}, s32[1,256]{1,0:T(1,128)S(1)}) custom-call(s32[1,64]{1,0:T(1,128)S(1)} %get-tuple-element.13.run_row_ref, s32[64,1]{1,0:T(8,128)S(1)} %copy.10.run_col_ref, s32[16]{0:T(128)S(1)} %copy-done), custom_call_target="tpu_custom_call" | custom-call | flops 16777216 | bytes 262144 | tf_op jit(solution)/shard_map/pallas_call | solution.py:314
  21.9 19.0 %all-to-all-done = bf16[256,5,2,128]{3,2,1,0:T(2,128)(2,1)S(1)} async-done(((bf16[256,5,2,128]{3,2,1,0:T(2,128)(2,1)}), bf16[256,5,2,128]{3,2,1,0:T(2,128)(2,1)S(1)}, u32[]{:S(2)}, u32[]{:S(2)}) %all-to-all-start) | async-done | bytes 655392 | tf_op jit(solution)/shard_map/all_to_all | solution.py:293
  41.0 0.6 shard_map.95
  41.6 22.3 %all_to_all.20 = bf16[32,8,2048]{2,1,0:T(8,128)(2,1)S(1)} all-to-all(bf16[32,8,2048]{2,1,0:T(8,128)(2,1)S(1)} %bitcast.11), channel_id=1, replica_groups=mesh['z_hi'=4,'core'=2,'y'=4,'z_lo'=2,'x'=4] {'y','x','core'}, dimensions={0} | all-to-all | bytes 2097152 | tf_op jit(solution)/shard_map/all_to_all | solution.py:293
  63.9 3.8 %shard_map.96 = bf16[256,2048]{1,0:T(8,128)(2,1)S(1)} custom-call(s32[1,256]{1,0:T(1,128)S(1)} %get-tuple-element.8.begin_ref, bf16[256,2048]{1,0:T(8,128)(2,1)S(1)} %bitcast.12), custom_call_target="tpu_custom_call" | custom-call | tf_op jit(solution)/shard_map/pallas_call | solution.py:282
  67.7 20.7 %all_to_all.21.r_ref = bf16[32,8,2048]{2,1,0:T(8,128)(2,1)S(1)} all-to-all(bf16[32,8,2048]{2,1,0:T(8,128)(2,1)S(1)} %bitcast.13), channel_id=1, replica_groups=mesh['z_hi'=4,'core'=2,'y'=4,'z_lo'=2,'x'=4] {'y','x','core'}, dimensions={0} | all-to-all | bytes 2097152 | tf_op jit(solution)/shard_map/all_to_all | solution.py:293
  88.4 0.4 shard_map.97
  88.8 27.9 %all_to_all.22 = bf16[256,5,2,128]{3,2,1,0:T(2,128)(2,1)S(1)} all-to-all(bf16[256,5,2,128]{3,2,1,0:T(2,128)(2,1)S(1)} %bitcast.14), channel_id=1, replica_groups=mesh['z_hi'=4,'core'=2,'y'=4,'z_lo'=2,'x'=4] {'z_hi','z_lo','y','x','core'}, dimensions={0} | all-to-all | bytes 1310720 | tf_op jit(solution)/shard_map/all_to_all | solution.py:293
  116.7 1.3 %shard_map.98 = (bf16[30,4096]{1,0:T(8,128)(2,1)}, bf16[30,4096]{1,0:T(8,128)(2,1)}, bf16[30,1024]{1,0:T(8,128)(2,1)}, bf16[30,1024]{1,0:T(8,128)(2,1)}) custom-call(bf16[2560,128]{1,0:T(8,128)(2,1)S(1)} %bitcast.15, bf16[320,320]{1,0:T(8,128)(2,1)S(1)} %get-tuple-element.11.place_ref), custom_call_target="tpu_custom_call" | custom-call | tf_op jit(solution)/shard_map/pallas_call | solution.py:282
  (2 shorter events, 0.0 us)
Async XLA Ops:
  3.0 37.9 %all-to-all-start = ((bf16[256,5,2,128]{3,2,1,0:T(2,128)(2,1)}), bf16[256,5,2,128]{3,2,1,0:T(2,128)(2,1)S(1)}, u32[]{:S(2)}, u32[]{:S(2)}) async-start(bf16[256,5,2,128]{3,2,1,0:T(2,128)(2,1)} %bitcast.17), calls=%async_computation | async-start | bytes 1310720 | tf_op jit(solution)/shard_map/all_to_all | solution.py:293
  19.7 0.7 copy-start

commit v7 on v6

--- a/solution.py
+++ b/solution.py
@@ -97,7 +97,7 @@
         copy.wait()
 
 
-def unpack_kernel(r_ref, place_ref, att_ref, gq_ref, gk_ref, gv_ref, qs, ks, vs, gs, x_ref, sem):
+def unpack_kernel(r_ref, place_ref, att_ref, gq_ref, gk_ref, gv_ref, qs, ks, vs, gs, sem):
     size = UNIT * 32
     pairs, half = KVH // 2, KVH * GROUP * HD // 2
     departures = []
@@ -107,10 +107,8 @@
         departures[-1].start()
 
     for pair in range(pairs):
-        two = pl.ds(pair * 2 * HD, 2 * HD)
-        for head in (2 * pair, 2 * pair + 1):
-            x_ref[:, pl.ds(head * HD, HD)] = r_ref[pl.ds(head * size, size), :]
-        rows = dot(place_ref[...], x_ref[:, two]).astype(bf16)
+        units = [r_ref[pl.ds((2 * pair + i) * size, size), :] for i in range(2)]
+        rows = dot(place_ref[...], jnp.concatenate(units, axis=1)).astype(bf16)
         for head in (2 * pair, 2 * pair + 1):
             part = rows[:, :HD] if head % 2 == 0 else rows[:, HD:]
             to = pl.ds(head * HD, HD)
@@ -168,14 +166,16 @@
     unpack_ref[...] = place_spread(False)
 
 
-def sort_kernel(r_ref, place_ref, out_ref, wide_ref, x_ref):
+def sort_kernel(r_ref, place_ref, out_ref, wide_ref):
     wide_ref[pl.ds(0, UNIT * BLOCK), :] = r_ref[...].astype(f32)
-    for u in range(UNIT):
-        x_ref[:, pl.ds(u * HD, HD)] = wide_ref[pl.ds(u, BLOCK, stride=UNIT), :].astype(bf16)
-    out_ref[:, pl.ds(0, 1280)] = dot(place_ref[pl.ds(0, BLOCK), :], x_ref[...]).astype(bf16)
+    units = [wide_ref[pl.ds(u, BLOCK, stride=UNIT), :].astype(bf16) for u in range(UNIT)]
+    pairs = [jnp.concatenate(units[u : u + 2], axis=1) for u in range(0, UNIT, 2)]
+    for i, pair in enumerate(pairs):
+        rows = dot(place_ref[pl.ds(0, BLOCK), :], pair)
+        out_ref[:, pl.ds(2 * HD * i, 2 * HD)] = rows.astype(bf16)
     for b in range(1, BACK + 1):
         out_ref[:, pl.ds(1024 + 256 * b, 256)] = dot(
-            place_ref[pl.ds(b * BLOCK, BLOCK), :], x_ref[:, pl.ds(1024, 256)]
+            place_ref[pl.ds(b * BLOCK, BLOCK), :], pairs[-1]
         ).astype(bf16)
 
 
@@ -336,7 +336,7 @@
     (ordered,) = call(
         sort_kernel,
         [(BLOCK, 2048)],
-        [pltpu.VMEM((units + 16, HD), f32), pltpu.VMEM((BLOCK, 1280), bf16)],
+        [pltpu.VMEM((units + 16, HD), f32)],
         spread,
         place_sort,
     )
@@ -373,7 +373,7 @@
         call(
             unpack_kernel,
             [wide, wide, narrow, narrow],
-            local + [pltpu.VMEM((size, KVH * HD), bf16), pltpu.SemaphoreType.DMA((6,))],
+            local + [pltpu.SemaphoreType.DMA((6,))],
             home,
             place_unpack,
             place_out=ANY,

time: 118 us -> 118 us (level)
  no operation moved by 1% of the time
where the time goes in v7:
time: 118 us
  blocking collectives  70.9 us (60%)
  waiting for transfers between devices  19 us (16%)
  starting transfers between devices  15.7 us (13%)
  Pallas kernels  9.9 us (8%)
  local copies, waits for them, and re-layouts  1.65 us (1%)
    all_to_all x3, blocking collectives, exchange(): return lax.all_to_all(x, axes, split_axis=0, concat_axis=0, tiled=True)  70.9 us
    all_to_all x1, waiting for transfers between devices, exchange(): return lax.all_to_all(x, axes, split_axis=0, concat_axis=0, tiled=True)  19 us
    all_to_all x1, starting transfers between devices, exchange(): return lax.all_to_all(x, axes, split_axis=0, concat_axis=0, tiled=True)  15.7 us
    pallas_call x5, Pallas kernels, call(): pl.pallas_call(kernel, out_shape=[jax.ShapeDtypeStruct(o, bf16) for o in...  8.33 us
  transfers between devices with their start and end apart: 1, of which 1 were waited for; matrix products, arithmetic and copies ran while one was open for 1% of the time, Pallas kernels for 1%

profile of v7, /device:TPU:1, one launch (start us, length us, event | category | flops | bytes accessed | tf_op | source)
XLA Modules:
  0.0 117.8 jit_solution(499690752313629375)
XLA Ops:
  0.6 2.4 %shard_map.94 = bf16[2560,128]{1,0:T(8,128)(2,1)} custom-call(bf16[30,4096]{1,0:T(8,128)(2,1)} %q_ref.1, bf16[30,1024]{1,0:T(8,128)(2,1)} %k_ref.1, bf16[30,1024]{1,0:T(8,128)(2,1)} %v_ref.1, bf16[30,4096]{1,0:T(8,128)(2,1)} %g_ref.1), custom_call_target="tpu_custom_call" | custom-call | tf_op jit(solution)/shard_map/pallas_call | solution.py:282
  3.0 15.7 %all-to-all-start = ((bf16[256,5,2,128]{3,2,1,0:T(2,128)(2,1)}), bf16[256,5,2,128]{3,2,1,0:T(2,128)(2,1)S(1)}, u32[]{:S(2)}, u32[]{:S(2)}) async-start(bf16[256,5,2,128]{3,2,1,0:T(2,128)(2,1)} %bitcast.17), calls=%async_computation | async-start | bytes 1310720 | tf_op jit(solution)/shard_map/all_to_all | solution.py:293
  18.7 0.9 slice.3
  19.6 0.1 copy.10.run_col_ref
  19.7 0.0 copy-start
  19.7 0.7 copy-done
  20.4 1.6 %shard_map.93 = (bf16[1024,256]{1,0:T(8,128)(2,1)S(1)}, bf16[256,256]{1,0:T(8,128)(2,1)S(1)}, bf16[320,320]{1,0:T(8,128)(2,1)S(1)}, s32[1,256]{1,0:T(1,128)S(1)}) custom-call(s32[1,64]{1,0:T(1,128)S(1)} %get-tuple-element.13.run_row_ref, s32[64,1]{1,0:T(8,128)S(1)} %copy.10.run_col_ref, s32[16]{0:T(128)S(1)} %copy-done), custom_call_target="tpu_custom_call" | custom-call | flops 16777216 | bytes 262144 | tf_op jit(solution)/shard_map/pallas_call | solution.py:314
  21.9 19.0 %all-to-all-done = bf16[256,5,2,128]{3,2,1,0:T(2,128)(2,1)S(1)} async-done(((bf16[256,5,2,128]{3,2,1,0:T(2,128)(2,1)}), bf16[256,5,2,128]{3,2,1,0:T(2,128)(2,1)S(1)}, u32[]{:S(2)}, u32[]{:S(2)}) %all-to-all-start) | async-done | bytes 655392 | tf_op jit(solution)/shard_map/all_to_all | solution.py:293
  41.0 0.5 shard_map.95
  41.5 22.4 %all_to_all.20 = bf16[32,8,2048]{2,1,0:T(8,128)(2,1)S(1)} all-to-all(bf16[32,8,2048]{2,1,0:T(8,128)(2,1)S(1)} %bitcast.11), channel_id=1, replica_groups=mesh['z_hi'=4,'core'=2,'y'=4,'z_lo'=2,'x'=4] {'y','x','core'}, dimensions={0} | all-to-all | bytes 2097152 | tf_op jit(solution)/shard_map/all_to_all | solution.py:293
  63.9 3.8 %shard_map.96 = bf16[256,2048]{1,0:T(8,128)(2,1)S(1)} custom-call(s32[1,256]{1,0:T(1,128)S(1)} %get-tuple-element.8.begin_ref, bf16[256,2048]{1,0:T(8,128)(2,1)S(1)} %bitcast.12), custom_call_target="tpu_custom_call" | custom-call | tf_op jit(solution)/shard_map/pallas_call | solution.py:282
  67.7 20.7 %all_to_all.21.r_ref = bf16[32,8,2048]{2,1,0:T(8,128)(2,1)S(1)} all-to-all(bf16[32,8,2048]{2,1,0:T(8,128)(2,1)S(1)} %bitcast.13), channel_id=1, replica_groups=mesh['z_hi'=4,'core'=2,'y'=4,'z_lo'=2,'x'=4] {'y','x','core'}, dimensions={0} | all-to-all | bytes 2097152 | tf_op jit(solution)/shard_map/all_to_all | solution.py:293
  88.3 0.4 shard_map.97
  88.7 27.9 %all_to_all.22 = bf16[256,5,2,128]{3,2,1,0:T(2,128)(2,1)S(1)} all-to-all(bf16[256,5,2,128]{3,2,1,0:T(2,128)(2,1)S(1)} %bitcast.14), channel_id=1, replica_groups=mesh['z_hi'=4,'core'=2,'y'=4,'z_lo'=2,'x'=4] {'z_hi','z_lo','y','x','core'}, dimensions={0} | all-to-all | bytes 1310720 | tf_op jit(solution)/shard_map/all_to_all | solution.py:293
  116.6 1.2 %shard_map.98 = (bf16[30,4096]{1,0:T(8,128)(2,1)}, bf16[30,4096]{1,0:T(8,128)(2,1)}, bf16[30,1024]{1,0:T(8,128)(2,1)}, bf16[30,1024]{1,0:T(8,128)(2,1)}) custom-call(bf16[2560,128]{1,0:T(8,128)(2,1)S(1)} %bitcast.15, bf16[320,320]{1,0:T(8,128)(2,1)S(1)} %get-tuple-element.11.place_ref), custom_call_target="tpu_custom_call" | custom-call | tf_op jit(solution)/shard_map/pallas_call | solution.py:282
  (2 shorter events, 0.0 us)
Async XLA Ops:
  3.0 37.9 %all-to-all-start = ((bf16[256,5,2,128]{3,2,1,0:T(2,128)(2,1)}), bf16[256,5,2,128]{3,2,1,0:T(2,128)(2,1)S(1)}, u32[]{:S(2)}, u32[]{:S(2)}) async-start(bf16[256,5,2,128]{3,2,1,0:T(2,128)(2,1)} %bitcast.17), calls=%async_computation | async-start | bytes 1310720 | tf_op jit(solution)/shard_map/all_to_all | solution.py:293
  19.7 0.7 copy-start
